TPU v7x, 512 devices: a whole 4x4x16 slice. The times are simulated.
512 devices in a mesh: blk: 32 (over x, y, z_hi), grp: 16 (over z_lo, core).
Axes of the slice: x: 4, y: 4, z: 16 (z_hi: 2, z_lo: 8; z = z_hi * 8 + z_lo), core: 2. Of those that a mesh axis runs over, the one named last changes fastest.
Arguments:
- images: bfloat16 [131072, 1152], P(('blk', 'grp')), may hold values from -1.796875 to 1.796875
- texts: bfloat16 [131072, 1152], P(('blk', 'grp')), may hold values from -1.796875 to 1.796875
- log_temp: float32 [1], replicated, may hold values from -0.5 to 0.5
- bias: float32 [1], replicated, may hold values from -3 to 0
Outputs:
- image_grad: bfloat16 [131072, 1152], P(('blk', 'grp'))
- text_grad: bfloat16 [131072, 1152], P(('blk', 'grp'))
- bias_grad: float32 [1], replicated
- temp_grad: float32 [1], replicated
All inputs are finite; a program needn't handle non-finite values.
Results may differ from a plain program's by a relative error of at most 0.0034.
Values may be sent and summed in bfloat16 or wider, within the bound.
No kernel may reach another device: no remote copies, remote signals or barrier semaphores. Data moves between devices by JAX's collectives and lax.ppermute only.
A program may use at most 64 MiB of HBM per device.

v0:
```python
import jax
import jax.numpy as jnp
from jax import lax
from jax.sharding import PartitionSpec as P


def passed_along(value, axis, steps):
    count = lax.axis_size(axis)
    pairs = [(source, (source + steps) % count) for source in range(count)]
    return lax.ppermute(value, axis, pairs)


def score_block(left, right, logit_scale, logit_bias, on_diagonal):
    products = lax.dot_general(
        left, right, (((1,), (1,)), ((), ())), preferred_element_type=jnp.float32
    )
    logits = logit_scale * products + logit_bias
    slopes = jax.nn.sigmoid(logits)
    if on_diagonal:
        slopes = slopes - jnp.eye(left.shape[0], dtype=jnp.float32)
    bias_part = jnp.sum(slopes)
    scale_part = jnp.sum(slopes * (logits - logit_bias))
    return (slopes.astype(jnp.bfloat16), bias_part, scale_part)


def grad_rows(half_slopes, right):
    return jnp.dot(half_slopes, right, preferred_element_type=jnp.float32)


def grad_cols(half_slopes, left):
    return lax.dot_general(
        half_slopes, left, (((0,), (0,)), ((), ())), preferred_element_type=jnp.float32
    )


def local(images, texts, log_temp, bias):
    logit_scale = jnp.exp(log_temp[0])
    logit_bias = bias[0]
    steps_count = lax.axis_size("blk") // 8
    own_slopes, bias_total, scale_total = score_block(images, texts, logit_scale, logit_bias, True)
    grad_left = grad_rows(own_slopes, texts)
    grad_right = grad_cols(own_slopes, images)
    near_images, near_texts = (images, texts)
    for offset in range(1, steps_count + 1):
        near_images, near_texts = passed_along((near_images, near_texts), "blk", -1)
        fore_slopes, bias_part, scale_part = score_block(
            images, near_texts, logit_scale, logit_bias, False
        )
        back_slopes, bias_more, scale_more = score_block(
            near_images, texts, logit_scale, logit_bias, False
        )
        bias_total = bias_total + bias_part + bias_more
        scale_total = scale_total + scale_part + scale_more
        grad_left = grad_left + grad_rows(fore_slopes, near_texts)
        grad_right = grad_right + grad_cols(back_slopes, near_images)
        away_left = grad_rows(back_slopes, texts)
        away_right = grad_cols(fore_slopes, images)
        back_left, back_right = passed_along((away_left, away_right), "blk", offset)
        grad_left = grad_left + back_left
        grad_right = grad_right + back_right
    bias_sum, scale_sum = lax.psum((bias_total, scale_total), ("blk", "grp"))
    batch_rows = images.shape[0] * lax.axis_size("blk") * lax.axis_size("grp")
    image_grad = (logit_scale * grad_left).astype(jnp.bfloat16)
    text_grad = (logit_scale * grad_right).astype(jnp.bfloat16)
    bias_grad = (bias_sum / batch_rows).reshape(1)
    temp_grad = (scale_sum / batch_rows).reshape(1)
    return (image_grad, text_grad, bias_grad, temp_grad)


def solution(mesh):
    in_specs = (P(("blk", "grp"), None), P(("blk", "grp"), None), P(), P())
    out_specs = (P(("blk", "grp"), None), P(("blk", "grp"), None), P(), P())
    return jax.shard_map(local, mesh=mesh, in_specs=in_specs, out_specs=out_specs, check_vma=False)
```

profile of v0, /device:TPU:1, one launch (start us, length us, event | category | flops | bytes accessed | tf_op | source)
XLA Modules:
  0.0 1023.3 jit_solution(18440248587548276356)
XLA Ops:
  0.6 20.9 %collective-permute-start = (bf16[256,1152]{1,0:T(8,128)(2,1)}, bf16[256,1152]{1,0:T(8,128)(2,1)}, u32[]{:S(2)}, u32[]{:S(2)}) collective-permute-start(bf16[256,1152]{1,0:T(8,128)(2,1)} %param.5), channel_id=1, source_target_pairs={{0,496},{16,0},{32,16},{48,32},{64,48},{80,64},{96,80},{112,96},{1... | collective-permute-start | bytes 1769480 | tf_op jit(solution)/shard_map/ppermute | solution.py:10
  21.6 1.9 collective-permute-start.1
  24.8 2.4 multiply_reduce_fusion.8
  27.2 0.4 fusion.45
  27.6 0.6 copy-done.1
  28.3 0.4 fusion.47
  28.6 9.6 collective-permute-done
  38.2 17.2 %collective-permute-start.3 = (bf16[256,1152]{1,0:T(8,128)(2,1)}, bf16[256,1152]{1,0:T(8,128)(2,1)}, u32[]{:S(2)}, u32[]{:S(2)}) collective-permute-start(bf16[256,1152]{1,0:T(8,128)(2,1)} %collective-permute-done), channel_id=1, source_target_pairs={{0,496},{16,0},{32,16},{48,32},{64,48},{80,64},{96,80},{112,96},{1... | collective-permute-start | bytes 1769480 | tf_op jit(solution)/shard_map/ppermute | solution.py:10
  55.3 2.1 multiply_reduce_fusion.7
  57.5 1.5 fusion.42
  58.9 1.9 collective-permute-start.12
  60.8 0.0 collective-permute-done.1
  60.9 21.4 %collective-permute-start.4 = (bf16[256,1152]{1,0:T(8,128)(2,1)}, bf16[256,1152]{1,0:T(8,128)(2,1)}, u32[]{:S(2)}, u32[]{:S(2)}) collective-permute-start(bf16[256,1152]{1,0:T(8,128)(2,1)} %collective-permute-done.1), channel_id=1, source_target_pairs={{0,496},{16,0},{32,16},{48,32},{64,48},{80,64},{96,80},{112,96},{1... | collective-permute-start | bytes 1769480 | tf_op jit(solution)/shard_map/ppermute | solution.py:10
  82.2 2.1 multiply_reduce_fusion.6
  84.4 0.7 copy-done.15
  85.1 1.4 fusion.40
  86.4 1.9 collective-permute-start.2
  92.0 0.0 collective-permute-done.3
  92.0 16.3 %collective-permute-start.6 = (bf16[256,1152]{1,0:T(8,128)(2,1)}, bf16[256,1152]{1,0:T(8,128)(2,1)}, u32[]{:S(2)}, u32[]{:S(2)}) collective-permute-start(bf16[256,1152]{1,0:T(8,128)(2,1)} %collective-permute-done.3), channel_id=1, source_target_pairs={{0,496},{16,0},{32,16},{48,32},{64,48},{80,64},{96,80},{112,96},{1... | collective-permute-start | bytes 1769480 | tf_op jit(solution)/shard_map/ppermute | solution.py:10
  108.3 2.2 multiply_reduce_fusion.5
  110.5 1.4 fusion.36
  111.9 1.9 collective-permute-start.13
  113.8 60.6 %collective-permute-done.4 = bf16[256,1152]{1,0:T(8,128)(2,1)} collective-permute-done((bf16[256,1152]{1,0:T(8,128)(2,1)}, bf16[256,1152]{1,0:T(8,128)(2,1)}, u32[]{:S(2)}, u32[]{:S(2)}) %collective-permute-start.4) | collective-permute-done | bytes 589856 | tf_op jit(solution)/shard_map/ppermute | solution.py:10
  174.5 2.2 multiply_reduce_fusion.4
  176.6 0.7 copy-done.5
  177.3 1.4 fusion.34
  178.7 1.9 collective-permute-start.5
  183.2 458.5 %collective-permute-done.6 = bf16[256,1152]{1,0:T(8,128)(2,1)} collective-permute-done((bf16[256,1152]{1,0:T(8,128)(2,1)}, bf16[256,1152]{1,0:T(8,128)(2,1)}, u32[]{:S(2)}, u32[]{:S(2)}) %collective-permute-start.6) | collective-permute-done | bytes 589856 | tf_op jit(solution)/shard_map/ppermute | solution.py:10
  641.7 17.0 %collective-permute-start.7 = (bf16[256,1152]{1,0:T(8,128)(2,1)}, bf16[256,1152]{1,0:T(8,128)(2,1)}, u32[]{:S(2)}, u32[]{:S(2)}) collective-permute-start(bf16[256,1152]{1,0:T(8,128)(2,1)} %collective-permute-done.4), channel_id=1, source_target_pairs={{0,496},{16,0},{32,16},{48,32},{64,48},{80,64},{96,80},{112,96},{1... | collective-permute-start | bytes 1769480 | tf_op jit(solution)/shard_map/ppermute | solution.py:10
  658.7 2.2 multiply_reduce_fusion.3
  660.9 0.7 copy-done.7
  661.6 1.4 fusion.30
  663.0 0.0 collective-permute-done.12
  663.1 2.0 collective-permute-start.14
  665.1 2.9 fusion.5
  668.0 49.0 %collective-permute-done.7 = bf16[256,1152]{1,0:T(8,128)(2,1)} collective-permute-done((bf16[256,1152]{1,0:T(8,128)(2,1)}, bf16[256,1152]{1,0:T(8,128)(2,1)}, u32[]{:S(2)}, u32[]{:S(2)}) %collective-permute-start.7) | collective-permute-done | bytes 589856 | tf_op jit(solution)/shard_map/ppermute | solution.py:10
  717.0 6.2 collective-permute-start.9
  723.2 0.0 collective-permute-done.2
  723.2 1.9 collective-permute-start.10
  725.1 1.8 fusion
  726.9 2.1 multiply_reduce_fusion.2
  729.0 1.4 fusion.28
  733.0 22.0 %collective-permute-done.9 = bf16[256,1152]{1,0:T(8,128)(2,1)} collective-permute-done((bf16[256,1152]{1,0:T(8,128)(2,1)}, bf16[256,1152]{1,0:T(8,128)(2,1)}, u32[]{:S(2)}, u32[]{:S(2)}) %collective-permute-start.9) | collective-permute-done | bytes 589856 | tf_op jit(solution)/shard_map/ppermute | solution.py:10
  754.9 24.8 %collective-permute-start.8 = (f32[256,1152]{1,0:T(8,128)}, f32[256,1152]{1,0:T(8,128)}, u32[]{:S(2)}, u32[]{:S(2)}) collective-permute-start(f32[256,1152]{1,0:T(8,128)} %fusion.28), channel_id=1, source_target_pairs={{0,48},{16,64},{32,80},{48,96},{64,112},{80,128},{96,144},{112,160... | collective-permute-start | bytes 3538952 | tf_op jit(solution)/shard_map/ppermute | solution.py:10
  779.8 2.1 multiply_reduce_fusion.1
  782.6 0.0 collective-permute-done.10
  782.6 2.8 multiply_reduce_fusion
  787.4 1.5 fusion.24
  788.9 10.7 %collective-permute-start.15 = (f32[256,1152]{1,0:T(8,128)}, f32[256,1152]{1,0:T(8,128)}, u32[]{:S(2)}, u32[]{:S(2)}) collective-permute-start(f32[256,1152]{1,0:T(8,128)} %fusion.24), channel_id=1, source_target_pairs={{0,64},{16,80},{32,96},{48,112},{64,128},{80,144},{96,160},{112,17... | collective-permute-start | bytes 3538952 | tf_op jit(solution)/shard_map/ppermute | solution.py:10
  799.5 184.1 %all-reduce = (f32[]{:T(128)}, f32[]{:T(128)}) all-reduce(f32[]{:T(128)S(6)} %add.207, f32[]{:T(128)S(6)} %add.215), channel_id=1, replica_groups=mesh['blk'=32,'grp'=16] {'blk','grp'}, use_global_device_ids=true, to_apply=%region_9.0 | all-reduce | flops 2 | bytes 16 | tf_op jit(solution)/shard_map/psum | solution.py:61
  984.9 1.3 fusion.22
  986.3 0.0 copy-start.4
  986.3 0.0 collective-permute-done.13
  986.3 3.3 collective-permute-start.11
  989.7 1.9 fusion.6
  991.6 1.9 fusion.1
  993.4 1.9 fusion.7
  995.4 0.0 copy-start.17
  995.4 0.0 collective-permute-done.8
  995.4 1.8 fusion.2
  997.2 0.0 collective-permute-done.15
  997.3 2.7 fusion.10
  1000.0 18.8 %collective-permute-done.11 = f32[256,1152]{1,0:T(8,128)S(1)} collective-permute-done((f32[256,1152]{1,0:T(8,128)S(1)}, f32[256,1152]{1,0:T(8,128)S(1)}, u32[]{:S(2)}, u32[]{:S(2)}) %collective-permute-start.11) | collective-permute-done | bytes 1179680 | tf_op jit(solution)/shard_map/ppermute | solution.py:10
  1018.8 2.2 fusion.11
  (32 shorter events, 0.1 us)
Async XLA Ops:
  0.6 37.6 %collective-permute-start = (bf16[256,1152]{1,0:T(8,128)(2,1)}, bf16[256,1152]{1,0:T(8,128)(2,1)}, u32[]{:S(2)}, u32[]{:S(2)}) collective-permute-start(bf16[256,1152]{1,0:T(8,128)(2,1)} %param.5), channel_id=1, source_target_pairs={{0,496},{16,0},{32,16},{48,32},{64,48},{80,64},{96,80},{112,96},{1... | collective-permute-start | bytes 1769480 | tf_op jit(solution)/shard_map/ppermute | solution.py:10
  21.6 39.3 %collective-permute-start.1 = (bf16[256,1152]{1,0:T(8,128)(2,1)}, bf16[256,1152]{1,0:T(8,128)(2,1)}, u32[]{:S(2)}, u32[]{:S(2)}) collective-permute-start(bf16[256,1152]{1,0:T(8,128)(2,1)} %param.4), channel_id=1, source_target_pairs={{0,496},{16,0},{32,16},{48,32},{64,48},{80,64},{96,80},{112,96},{1... | collective-permute-start | bytes 1769480 | tf_op jit(solution)/shard_map/ppermute | solution.py:10
  24.8 2.4 copy-start
  27.2 1.1 copy-start.1
  38.2 53.8 %collective-permute-start.3 = (bf16[256,1152]{1,0:T(8,128)(2,1)}, bf16[256,1152]{1,0:T(8,128)(2,1)}, u32[]{:S(2)}, u32[]{:S(2)}) collective-permute-start(bf16[256,1152]{1,0:T(8,128)(2,1)} %collective-permute-done), channel_id=1, source_target_pairs={{0,496},{16,0},{32,16},{48,32},{64,48},{80,64},{96,80},{112,96},{1... | collective-permute-start | bytes 1769480 | tf_op jit(solution)/shard_map/ppermute | solution.py:10
  57.5 26.9 %copy-start.9 = (f32[256,256]{1,0:T(8,128)}, f32[256,256]{1,0:T(8,128)S(1)}, u32[]{:S(2)}) copy-start(f32[256,256]{1,0:T(8,128)S(1)} %get-tuple-element.25) | copy-start | bytes 786436
  58.9 604.1 %collective-permute-start.12 = (f32[256,1152]{1,0:T(8,128)}, f32[256,1152]{1,0:T(8,128)}, u32[]{:S(2)}, u32[]{:S(2)}) collective-permute-start(f32[256,1152]{1,0:T(8,128)} %fusion.42), channel_id=1, source_target_pairs={{0,16},{16,32},{32,48},{48,64},{64,80},{80,96},{96,112},{112,128},... | collective-permute-start | bytes 3538952 | tf_op jit(solution)/shard_map/ppermute | solution.py:10
  60.9 113.6 %collective-permute-start.4 = (bf16[256,1152]{1,0:T(8,128)(2,1)}, bf16[256,1152]{1,0:T(8,128)(2,1)}, u32[]{:S(2)}, u32[]{:S(2)}) collective-permute-start(bf16[256,1152]{1,0:T(8,128)(2,1)} %collective-permute-done.1), channel_id=1, source_target_pairs={{0,496},{16,0},{32,16},{48,32},{64,48},{80,64},{96,80},{112,96},{1... | collective-permute-start | bytes 1769480 | tf_op jit(solution)/shard_map/ppermute | solution.py:10
  84.3 0.7 copy-start.15
  86.4 636.7 %collective-permute-start.2 = (f32[256,1152]{1,0:T(8,128)}, f32[256,1152]{1,0:T(8,128)}, u32[]{:S(2)}, u32[]{:S(2)}) collective-permute-start(f32[256,1152]{1,0:T(8,128)} %fusion.40), channel_id=1, source_target_pairs={{0,16},{16,32},{32,48},{48,64},{64,80},{80,96},{96,112},{112,128},... | collective-permute-start | bytes 3538952 | tf_op jit(solution)/shard_map/ppermute | solution.py:10
  92.0 549.7 %collective-permute-start.6 = (bf16[256,1152]{1,0:T(8,128)(2,1)}, bf16[256,1152]{1,0:T(8,128)(2,1)}, u32[]{:S(2)}, u32[]{:S(2)}) collective-permute-start(bf16[256,1152]{1,0:T(8,128)(2,1)} %collective-permute-done.3), channel_id=1, source_target_pairs={{0,496},{16,0},{32,16},{48,32},{64,48},{80,64},{96,80},{112,96},{1... | collective-permute-start | bytes 1769480 | tf_op jit(solution)/shard_map/ppermute | solution.py:10
  110.5 66.1 %copy-start.3 = (f32[256,256]{1,0:T(8,128)}, f32[256,256]{1,0:T(8,128)S(1)}, u32[]{:S(2)}) copy-start(f32[256,256]{1,0:T(8,128)S(1)} %get-tuple-element.27) | copy-start | bytes 786436
  111.9 874.4 %collective-permute-start.13 = (f32[256,1152]{1,0:T(8,128)}, f32[256,1152]{1,0:T(8,128)}, u32[]{:S(2)}, u32[]{:S(2)}) collective-permute-start(f32[256,1152]{1,0:T(8,128)} %fusion.36), channel_id=1, source_target_pairs={{0,32},{16,48},{32,64},{48,80},{64,96},{80,112},{96,128},{112,144}... | collective-permute-start | bytes 3538952 | tf_op jit(solution)/shard_map/ppermute | solution.py:10
  176.6 0.7 copy-start.5
  178.7 812.8 %collective-permute-start.5 = (f32[256,1152]{1,0:T(8,128)}, f32[256,1152]{1,0:T(8,128)}, u32[]{:S(2)}, u32[]{:S(2)}) collective-permute-start(f32[256,1152]{1,0:T(8,128)} %fusion.34), channel_id=1, source_target_pairs={{0,32},{16,48},{32,64},{48,80},{64,96},{80,112},{96,128},{112,144}... | collective-permute-start | bytes 3538952 | tf_op jit(solution)/shard_map/ppermute | solution.py:10
  641.7 75.3 %collective-permute-start.7 = (bf16[256,1152]{1,0:T(8,128)(2,1)}, bf16[256,1152]{1,0:T(8,128)(2,1)}, u32[]{:S(2)}, u32[]{:S(2)}) collective-permute-start(bf16[256,1152]{1,0:T(8,128)(2,1)} %collective-permute-done.4), channel_id=1, source_target_pairs={{0,496},{16,0},{32,16},{48,32},{64,48},{80,64},{96,80},{112,96},{1... | collective-permute-start | bytes 1769480 | tf_op jit(solution)/shard_map/ppermute | solution.py:10
  660.9 0.7 copy-start.7
  660.9 4.2 copy-start.16
  663.0 62.1 %copy-start.10 = (f32[256,256]{1,0:T(8,128)S(1)}, f32[256,256]{1,0:T(8,128)}, u32[]{:S(2)}) copy-start(f32[256,256]{1,0:T(8,128)} %copy-done.9) | copy-start | bytes 786436
  663.1 330.4 %collective-permute-start.14 = (f32[256,1152]{1,0:T(8,128)}, f32[256,1152]{1,0:T(8,128)}, u32[]{:S(2)}, u32[]{:S(2)}) collective-permute-start(f32[256,1152]{1,0:T(8,128)} %fusion.30), channel_id=1, source_target_pairs={{0,48},{16,64},{32,80},{48,96},{64,112},{80,128},{96,144},{112,160... | collective-permute-start | bytes 3538952 | tf_op jit(solution)/shard_map/ppermute | solution.py:10
  717.0 38.0 %collective-permute-start.9 = (bf16[256,1152]{1,0:T(8,128)(2,1)}, bf16[256,1152]{1,0:T(8,128)(2,1)}, u32[]{:S(2)}, u32[]{:S(2)}) collective-permute-start(bf16[256,1152]{1,0:T(8,128)(2,1)} %collective-permute-done.6), channel_id=1, source_target_pairs={{0,496},{16,0},{32,16},{48,32},{64,48},{80,64},{96,80},{112,96},{1... | collective-permute-start | bytes 1769480 | tf_op jit(solution)/shard_map/ppermute | solution.py:10
  723.2 59.4 %collective-permute-start.10 = (bf16[256,1152]{1,0:T(8,128)(2,1)}, bf16[256,1152]{1,0:T(8,128)(2,1)}, u32[]{:S(2)}, u32[]{:S(2)}) collective-permute-start(bf16[256,1152]{1,0:T(8,128)(2,1)} %collective-permute-done.7), channel_id=1, source_target_pairs={{0,496},{16,0},{32,16},{48,32},{64,48},{80,64},{96,80},{112,96},{1... | collective-permute-start | bytes 1769480 | tf_op jit(solution)/shard_map/ppermute | solution.py:10
  729.0 50.7 %copy-start.13 = (f32[256,256]{1,0:T(8,128)}, f32[256,256]{1,0:T(8,128)S(1)}, u32[]{:S(2)}) copy-start(f32[256,256]{1,0:T(8,128)S(1)} %get-tuple-element.30) | copy-start | bytes 786436
  754.9 240.4 %collective-permute-start.8 = (f32[256,1152]{1,0:T(8,128)}, f32[256,1152]{1,0:T(8,128)}, u32[]{:S(2)}, u32[]{:S(2)}) collective-permute-start(f32[256,1152]{1,0:T(8,128)} %fusion.28), channel_id=1, source_target_pairs={{0,48},{16,64},{32,80},{48,96},{64,112},{80,128},{96,144},{112,160... | collective-permute-start | bytes 3538952 | tf_op jit(solution)/shard_map/ppermute | solution.py:10
  781.9 5.5 copy-start.11
  788.9 200.8 %copy-start.2 = (f32[256,1152]{1,0:T(8,128)S(1)}, f32[256,1152]{1,0:T(8,128)}, u32[]{:S(2)}) copy-start(f32[256,1152]{1,0:T(8,128)} %fusion.5) | copy-start | bytes 3538948
  788.9 200.8 %copy-start.6 = (f32[256,256]{1,0:T(8,128)S(1)}, f32[256,256]{1,0:T(8,128)}, u32[]{:S(2)}) copy-start(f32[256,256]{1,0:T(8,128)} %copy-done.5) | copy-start | bytes 786436
  788.9 208.4 %collective-permute-start.15 = (f32[256,1152]{1,0:T(8,128)}, f32[256,1152]{1,0:T(8,128)}, u32[]{:S(2)}, u32[]{:S(2)}) collective-permute-start(f32[256,1152]{1,0:T(8,128)} %fusion.24), channel_id=1, source_target_pairs={{0,64},{16,80},{32,96},{48,112},{64,128},{80,144},{96,160},{112,17... | collective-permute-start | bytes 3538952 | tf_op jit(solution)/shard_map/ppermute | solution.py:10
  986.3 5.3 copy-start.4
  986.3 32.5 %collective-permute-start.11 = (f32[256,1152]{1,0:T(8,128)S(1)}, f32[256,1152]{1,0:T(8,128)S(1)}, u32[]{:S(2)}, u32[]{:S(2)}) collective-permute-start(f32[256,1152]{1,0:T(8,128)S(1)} %fusion.22), channel_id=1, source_target_pairs={{0,64},{16,80},{32,96},{48,112},{64,128},{80,144},{96,160},{112,17... | collective-permute-start | bytes 3538952 | tf_op jit(solution)/shard_map/ppermute | solution.py:10
  991.5 1.9 copy-start.14
  993.4 2.0 copy-start.8
  995.4 1.9 copy-start.17
  997.2 21.5 %copy-start.12 = (f32[256,256]{1,0:T(8,128)S(1)}, f32[256,256]{1,0:T(8,128)}, u32[]{:S(2)}) copy-start(f32[256,256]{1,0:T(8,128)} %copy-done.11) | copy-start | bytes 786436
where the time goes:
time: 1020 us
  waiting for transfers between devices  618 us (61%)
  blocking collectives  184 us (18%)
  starting transfers between devices  151 us (15%)
  matrix products  49.3 us (5%)
  between operations  17.3 us (2%)
    ppermute x16, waiting for transfers between devices, passed_along(): return lax.ppermute(value, axis, pairs)  618 us
    psum x1, blocking collectives, local(): bias_sum, scale_sum = lax.psum((bias_total, scale_total), ('blk', 'grp'))  184 us
    ppermute x16, starting transfers between devices, passed_along(): return lax.ppermute(value, axis, pairs)  151 us
  transfers between devices with their start and end apart: 16, of which 6 were waited for; matrix products, arithmetic and copies ran while one was open for 5% of the time, Pallas kernels for 0%

commit v1 on v0

v1 whole, which is shorter than its diff:
```python
import jax
import jax.numpy as jnp
from jax import lax
from jax.experimental import pallas as pl
from jax.experimental.pallas import tpu as pltpu
from jax.sharding import PartitionSpec as P

F32, BF16 = jnp.float32, jnp.bfloat16
CHUNKS = 2
VMEM = pl.BlockSpec(memory_space=pltpu.VMEM)
SMEM = pl.BlockSpec(memory_space=pltpu.SMEM)
PARAMS = pltpu.CompilerParams(vmem_limit_bytes=48 * 1024 * 1024)


def dot(left, right, left_dim, right_dim):
    return lax.dot_general(
        left, right, (((left_dim,), (right_dim,)), ((), ())), preferred_element_type=F32
    )


def fold(tile):
    return jnp.sum(tile.reshape(-1, 8, tile.shape[-1]), axis=0)


def score(scalars, texts, images, on_diagonal):
    products = dot(texts, images, 1, 1)
    slopes = jax.nn.sigmoid(scalars[0] * products + scalars[1])
    if on_diagonal:
        rows = lax.broadcasted_iota(jnp.int32, slopes.shape, 0)
        columns = lax.broadcasted_iota(jnp.int32, slopes.shape, 1)
        slopes = slopes - jnp.where(rows == columns, 1.0, 0.0)
    return slopes.astype(BF16), fold(slopes), fold(slopes * products)


def own_kernel(scalars, texts, mine, ahead, behind, outer, inner, slopes_out, grad_out, inner_out, sums_out):
    bias_sum = scale_sum = grad = None
    for slot, images in enumerate((mine, ahead, behind, outer, inner)):
        half, bias_part, scale_part = score(scalars, texts[...], images[...], slot == 0)
        part = dot(half, images[...], 1, 0)
        if slot == 0:
            bias_sum, scale_sum, grad = bias_part, scale_part, part
        else:
            bias_sum, scale_sum, grad = bias_sum + bias_part, scale_sum + scale_part, grad + part
        if slot == 4:
            inner_out[...] = dot(half, texts[...], 0, 0).astype(BF16)
        else:
            slopes_out[slot] = half
    grad_out[...] = grad
    sums_out[0:8] = bias_sum
    sums_out[8:16] = scale_sum


def far_kernel(scalars, texts, mine, ahead, behind, outer, sums_in, slopes_out, grad_out, sums_out):
    bias_sum, scale_sum, grad = sums_in[0:8], sums_in[8:16], None
    for slot, images in enumerate((mine, ahead, behind, outer)):
        half, bias_part, scale_part = score(scalars, texts[...], images[...], False)
        part = dot(half, images[...], 1, 0)
        grad = part if grad is None else grad + part
        bias_sum, scale_sum = bias_sum + bias_part, scale_sum + scale_part
        slopes_out[slot] = half
    grad_out[...] = grad.astype(BF16)
    sums_out[0:8] = bias_sum
    sums_out[8:16] = scale_sum


def images_kernel(texts, own_slopes, *refs):
    far_texts, far_slopes = refs[:CHUNKS], refs[CHUNKS : 2 * CHUNKS]
    outs = refs[2 * CHUNKS :]
    for slot in (1, 2, 3, 0):
        grad = dot(own_slopes[slot], texts[...], 0, 0)
        for part, slopes in zip(far_texts, far_slopes, strict=True):
            grad = grad + dot(slopes[slot], part[...], 0, 0)
        outs[slot][...] = grad.astype(outs[slot].dtype)


def shape(rows, columns, kind):
    return jax.ShapeDtypeStruct((rows, columns), kind)


def cost(pairs, rows, width, moved):
    return pl.CostEstimate(flops=2 * pairs * rows * rows * width, bytes_accessed=moved, transcendentals=0)


def local(images, texts, log_temp, bias):
    rows, width = images.shape
    n_blk = lax.axis_size("blk")
    world = n_blk * lax.axis_size("grp")
    scale = jnp.exp(log_temp[0])
    scalars = jnp.stack([scale, bias[0]])
    block = rows * width * 2

    flip = [(s, s ^ 1) for s in range(n_blk)]

    def columns(count):
        return [(s, (s - 2 * count) % n_blk) for s in range(n_blk)]

    outward = [(s, (s - 4 * (1 - 2 * (s % 2))) % n_blk) for s in range(n_blk)]

    def back(pairs):
        return [(b, a) for a, b in pairs]

    part_rows = rows // CHUNKS
    far_texts = [
        lax.ppermute(texts[i * part_rows : (i + 1) * part_rows], "blk", flip) for i in range(CHUNKS)
    ]
    ways = (columns(1), columns(-1), outward, back(outward))
    ahead, behind, outer, inner = [lax.ppermute(images, "blk", way) for way in ways]

    own_slopes, text_own, inner_part, sums = pl.pallas_call(
        own_kernel,
        out_shape=(
            jax.ShapeDtypeStruct((4, rows, rows), BF16),
            shape(rows, width, F32),
            shape(rows, width, BF16),
            shape(16, rows, F32),
        ),
        in_specs=[SMEM] + [VMEM] * 6,
        out_specs=(VMEM,) * 4,
        compiler_params=PARAMS,
        cost_estimate=cost(11, rows, width, 10 * block),
        name="own_pairs",
    )(scalars, texts, images, ahead, behind, outer, inner)
    inner_back = lax.ppermute(inner_part, "blk", back(ways[3]))

    far_slopes, text_back = [], []
    for part in far_texts:
        slopes, grad, sums = pl.pallas_call(
            far_kernel,
            out_shape=(
                jax.ShapeDtypeStruct((4, part_rows, rows), BF16),
                shape(part_rows, width, BF16),
                shape(16, rows, F32),
            ),
            in_specs=[SMEM] + [VMEM] * 6,
            out_specs=(VMEM,) * 3,
            compiler_params=PARAMS,
            cost_estimate=cost(8 // CHUNKS, rows, width, 6 * block),
            name="far_pairs",
        )(scalars, part, images, ahead, behind, outer, sums)
        far_slopes.append(slopes)
        text_back.append(lax.ppermute(grad, "blk", flip))

    image_own, ahead_part, behind_part, outer_part = pl.pallas_call(
        images_kernel,
        out_shape=(shape(rows, width, F32),) + (shape(rows, width, BF16),) * 3,
        in_specs=[VMEM] * (2 + 2 * CHUNKS),
        out_specs=(VMEM,) * 4,
        compiler_params=PARAMS,
        cost_estimate=cost(8, rows, width, 8 * block),
        name="image_parts",
    )(texts, own_slopes, *far_texts, *far_slopes)
    image_back = [
        lax.ppermute(part, "blk", back(way))
        for part, way in zip((ahead_part, behind_part, outer_part), ways[:3], strict=True)
    ]

    totals = jnp.sum(sums.reshape(2, -1), axis=1)
    row = jnp.pad(totals, (0, 126)).reshape(1, 128)
    shared = lax.all_to_all(jnp.tile(row, (world, 1)), ("blk", "grp"), 0, 0, tiled=True)
    sums_all = jnp.sum(shared, axis=0)
    batch_rows = rows * world
    bias_grad = (sums_all[0] / batch_rows).reshape(1)
    temp_grad = (scale * sums_all[1] / batch_rows).reshape(1)

    image_sum = image_own + inner_back.astype(F32)
    for part in image_back:
        image_sum = image_sum + part.astype(F32)
    image_grad = (scale * image_sum).astype(BF16)
    text_grad = (scale * (text_own + jnp.concatenate(text_back, axis=0).astype(F32))).astype(BF16)
    return image_grad, text_grad, bias_grad, temp_grad


def solution(mesh):
    in_specs = (P(("blk", "grp"), None), P(("blk", "grp"), None), P(), P())
    out_specs = (P(("blk", "grp"), None), P(("blk", "grp"), None), P(), P())
    return jax.shard_map(local, mesh=mesh, in_specs=in_specs, out_specs=out_specs, check_vma=False)
```

time: 1020 us -> 194 us (0.19)
  waiting for transfers between devices: 618 us -> 33.3 us
  blocking collectives: 184 us -> 0 us
  matrix products: 49.3 us -> 0 us
  starting transfers between devices: 151 us -> 132 us
  Pallas kernels: 0 us -> 12 us
  between operations: 17.3 us -> 5.71 us
    ppermute x16 -> x12, waiting for transfers between devices: 618 us -> 15.8 us  [the longest x2 14.7 us: local(): lax.ppermute(texts[i * part_rows:(i + 1) * part_rows], 'blk', flip)]
    psum x1 -> x0, blocking collectives: 184 us -> none  [local(): bias_sum, scale_sum = lax.psum((bias_total, scale_total), ('blk', 'grp'))]
    dot_general x27 -> x0, matrix products: 49.3 us -> none  [the longest x9 20.1 us: score_block(): lax.dot_general(left, right, (((1,), (1,)), ((), ())), preferred_element_...]
    ppermute x16 -> x12, starting transfers between devices: 151 us -> 103 us  [the longest x2 29.6 us: local(): lax.ppermute(texts[i * part_rows:(i + 1) * part_rows], 'blk', flip)]
    all_to_all x0 -> x1, starting transfers between devices: none -> 29.5 us  [local(): lax.all_to_all(jnp.tile(row, (world, 1)), ('blk', 'grp'), 0, 0, tiled=True)]
    all_to_all x0 -> x1, waiting for transfers between devices: none -> 17.5 us  [local(): lax.all_to_all(jnp.tile(row, (world, 1)), ('blk', 'grp'), 0, 0, tiled=True)]
    pallas_call x0 -> x4, Pallas kernels: none -> 12 us  [the longest x2 5.67 us: local(): pl.pallas_call(far_kernel, out_shape=(jax.ShapeDtypeStruct((4, part_rows,...]
  transfers between devices with their start and end apart: 16 -> 13, of which waited for: 6 -> 3; matrix products, arithmetic and copies ran while one was open for 5% -> 4% of each run, Pallas kernels for 0% -> 5%
where the time goes in v1:
time: 194 us; the launch traced here: 193 us
  starting transfers between devices  132 us (68%)
  waiting for transfers between devices  33.3 us (17%)
  Pallas kernels  12 us (6%)
  other arithmetic  6.64 us (3%)
  between operations  5.71 us (3%)
  local copies, waits for them, and re-layouts  3.27 us (2%)
    ppermute x2, starting transfers between devices, local(): lax.ppermute(texts[i * part_rows:(i + 1) * part_rows], 'blk', flip)  29.6 us
    all_to_all x1, starting transfers between devices, local(): lax.all_to_all(jnp.tile(row, (world, 1)), ('blk', 'grp'), 0, 0, tiled=True)  29.5 us
    ppermute x1, starting transfers between devices, local(): inner_back = lax.ppermute(inner_part, 'blk', back(ways[3]))  22.6 us
    ppermute x4, starting transfers between devices, local(): lax.ppermute(images, 'blk', way)  18.5 us
    ppermute x3, starting transfers between devices, local(): lax.ppermute(part, 'blk', back(way))  17.9 us
    all_to_all x1, waiting for transfers between devices, local(): lax.all_to_all(jnp.tile(row, (world, 1)), ('blk', 'grp'), 0, 0, tiled=True)  17.5 us
    ppermute x2, waiting for transfers between devices, local(): lax.ppermute(texts[i * part_rows:(i + 1) * part_rows], 'blk', flip)  14.7 us
    ppermute x2, starting transfers between devices, local(): text_back.append(lax.ppermute(grad, 'blk', flip))  14.3 us
  transfers between devices with their start and end apart: 13, of which 3 were waited for; matrix products, arithmetic and copies ran while one was open for 4% of the time, Pallas kernels for 5%

profile of v1, /device:TPU:1, one launch (start us, length us, event | category | flops | bytes accessed | tf_op | source)
XLA Modules:
  0.0 193.4 jit_solution(10299715353383660545)
XLA Ops:
  0.6 0.0 copy-start
  0.6 0.0 copy-start.1
  0.6 5.8 %collective-permute-start.3 = (bf16[256,1152]{1,0:T(8,128)(2,1)}, bf16[256,1152]{1,0:T(8,128)(2,1)S(1)}, u32[]{:S(2)}, u32[]{:S(2)}) collective-permute-start(bf16[256,1152]{1,0:T(8,128)(2,1)} %mine.5), channel_id=1, source_target_pairs={{448,0},{80,16},{480,32},{112,48},{0,64},{144,80},{32,96},{176,112... | collective-permute-start | bytes 1769480 | tf_op jit(solution)/shard_map/ppermute | solution.py:107
  6.4 4.1 %collective-permute-start.2 = (bf16[256,1152]{1,0:T(8,128)(2,1)}, bf16[256,1152]{1,0:T(8,128)(2,1)S(1)}, u32[]{:S(2)}, u32[]{:S(2)}) collective-permute-start(bf16[256,1152]{1,0:T(8,128)(2,1)} %mine.5), channel_id=1, source_target_pairs={{0,448},{16,80},{32,480},{48,112},{64,0},{80,144},{96,32},{112,176... | collective-permute-start | bytes 1769480 | tf_op jit(solution)/shard_map/ppermute | solution.py:107
  10.6 3.2 %collective-permute-start.1 = (bf16[256,1152]{1,0:T(8,128)(2,1)}, bf16[256,1152]{1,0:T(8,128)(2,1)S(1)}, u32[]{:S(2)}, u32[]{:S(2)}) collective-permute-start(bf16[256,1152]{1,0:T(8,128)(2,1)} %mine.5), channel_id=1, source_target_pairs={{0,32},{16,48},{32,64},{48,80},{64,96},{80,112},{96,128},{112,144}... | collective-permute-start | bytes 1769480 | tf_op jit(solution)/shard_map/ppermute | solution.py:107
  13.7 5.4 %collective-permute-start = (bf16[256,1152]{1,0:T(8,128)(2,1)}, bf16[256,1152]{1,0:T(8,128)(2,1)S(1)}, u32[]{:S(2)}, u32[]{:S(2)}) collective-permute-start(bf16[256,1152]{1,0:T(8,128)(2,1)} %mine.5), channel_id=1, source_target_pairs={{0,480},{16,496},{32,0},{48,16},{64,32},{80,48},{96,64},{112,80},{... | collective-permute-start | bytes 1769480 | tf_op jit(solution)/shard_map/ppermute | solution.py:107
  19.2 1.1 fusion
  20.3 15.6 %collective-permute-start.4 = (bf16[128,1152]{1,0:T(8,128)(2,1)S(1)}, bf16[128,1152]{1,0:T(8,128)(2,1)S(1)}, u32[]{:S(2)}, u32[]{:S(2)}) collective-permute-start(bf16[128,1152]{1,0:T(8,128)(2,1)S(1)} %get-tuple-element.33), channel_id=1, source_target_pairs={{0,16},{16,0},{32,48},{48,32},{64,80},{80,64},{96,112},{112,96},{1... | collective-permute-start | bytes 884744 | tf_op jit(solution)/shard_map/ppermute | solution.py:104
  37.2 0.0 collective-permute-done.3.inner
  37.2 14.0 %collective-permute-start.5 = (bf16[128,1152]{1,0:T(8,128)(2,1)S(1)}, bf16[128,1152]{1,0:T(8,128)(2,1)S(1)}, u32[]{:S(2)}, u32[]{:S(2)}) collective-permute-start(bf16[128,1152]{1,0:T(8,128)(2,1)S(1)} %get-tuple-element.32), channel_id=1, source_target_pairs={{0,16},{16,0},{32,48},{48,32},{64,80},{80,64},{96,112},{112,96},{1... | collective-permute-start | bytes 884744 | tf_op jit(solution)/shard_map/ppermute | solution.py:104
  51.2 0.1 pad_maximum_fusion.scalars
  51.3 0.0 collective-permute-done.2.outer
  51.3 0.0 collective-permute-done.1.behind
  51.3 1.1 collective-permute-done.ahead
  52.5 0.0 copy-done
  52.5 0.0 copy-done.1
  52.5 3.8 %own_pairs.1 = (bf16[4,256,256]{2,1,0:T(8,128)(2,1)S(1)}, f32[256,1152]{1,0:T(8,128)S(1)}, bf16[256,1152]{1,0:T(8,128)(2,1)S(1)}, f32[16,256]{1,0:T(8,128)S(1)}) custom-call(f32[2]{0:T(128)S(1)} %pad_maximum_fusion.scalars, bf16[256,1152]{1,0:T(8,128)(2,1)S(1)} %copy-done.1, bf16[256,1152]{1,0:T(8,128)(2,1)S(1)} %copy-done, ...), custom_call_target="tpu_custom_call" | custom-call | flops 1660944384 | bytes 5898240 | tf_op jit(solution)/shard_map/own_pairs/pallas_call | solution.py:109
  56.2 0.0 collective-permute-done.4.texts.refs_0_
  56.2 3.2 %far_pairs.2 = (bf16[4,128,256]{2,1,0:T(8,128)(2,1)S(1)}, bf16[128,1152]{1,0:T(8,128)(2,1)}, f32[16,256]{1,0:T(8,128)S(1)}) custom-call(f32[2]{0:T(128)S(1)} %pad_maximum_fusion.scalars, bf16[128,1152]{1,0:T(8,128)(2,1)S(1)} %collective-permute-done.4.texts.refs_0_, bf16[256,1152]{1,0:T(8,128)(2,1)S(1)} %copy-done, ...), custom_call_target="tpu_custom_call" | custom-call | flops 603979776 | bytes 3538944 | tf_op jit(solution)/shard_map/far_pairs/pallas_call | solution.py:127
  59.4 14.7 %collective-permute-done.5.texts.refs_1_ = bf16[128,1152]{1,0:T(8,128)(2,1)S(1)} collective-permute-done((bf16[128,1152]{1,0:T(8,128)(2,1)S(1)}, bf16[128,1152]{1,0:T(8,128)(2,1)S(1)}, u32[]{:S(2)}, u32[]{:S(2)}) %collective-permute-start.5) | collective-permute-done | bytes 294944 | tf_op jit(solution)/shard_map/ppermute | solution.py:104
  74.1 2.5 %far_pairs.3 = (bf16[4,128,256]{2,1,0:T(8,128)(2,1)S(1)}, bf16[128,1152]{1,0:T(8,128)(2,1)S(1)}, f32[16,256]{1,0:T(8,128)S(1)}) custom-call(f32[2]{0:T(128)S(1)} %pad_maximum_fusion.scalars, bf16[128,1152]{1,0:T(8,128)(2,1)S(1)} %collective-permute-done.5.texts.refs_1_, bf16[256,1152]{1,0:T(8,128)(2,1)S(1)} %copy-done, ...), custom_call_target="tpu_custom_call" | custom-call | flops 603979776 | bytes 3538944 | tf_op jit(solution)/shard_map/far_pairs/pallas_call | solution.py:127
  76.6 12.4 %collective-permute-start.11 = (bf16[128,1152]{1,0:T(8,128)(2,1)S(1)}, bf16[128,1152]{1,0:T(8,128)(2,1)S(1)}, u32[]{:S(2)}, u32[]{:S(2)}) collective-permute-start(bf16[128,1152]{1,0:T(8,128)(2,1)S(1)} %get-tuple-element.30), channel_id=1, source_target_pairs={{0,16},{16,0},{32,48},{48,32},{64,80},{80,64},{96,112},{112,96},{1... | collective-permute-start | bytes 884744 | tf_op jit(solution)/shard_map/ppermute | solution.py:141
  89.0 1.9 collective-permute-start.10
  90.9 22.6 %collective-permute-start.6 = (bf16[256,1152]{1,0:T(8,128)(2,1)S(1)}, bf16[256,1152]{1,0:T(8,128)(2,1)}, u32[]{:S(2)}, u32[]{:S(2)}) collective-permute-start(bf16[256,1152]{1,0:T(8,128)(2,1)S(1)} %get-tuple-element.24), channel_id=1, source_target_pairs={{0,448},{16,80},{32,480},{48,112},{64,0},{80,144},{96,32},{112,176... | collective-permute-start | bytes 1769480 | tf_op jit(solution)/shard_map/ppermute | solution.py:123
  113.5 2.6 %image_parts.1 = (f32[256,1152]{1,0:T(8,128)S(1)}, bf16[256,1152]{1,0:T(8,128)(2,1)}, bf16[256,1152]{1,0:T(8,128)(2,1)}, bf16[256,1152]{1,0:T(8,128)(2,1)S(1)}) custom-call(bf16[256,1152]{1,0:T(8,128)(2,1)S(1)} %copy-done.1, bf16[4,256,256]{2,1,0:T(8,128)(2,1)S(1)} %get-tuple-element.18.own_slopes, ...), custom_call_target="tpu_custom_call" | custom-call | flops 1207959552 | bytes 4718592 | tf_op jit(solution)/shard_map/image_parts/pallas_call | solution.py:143
  116.1 1.9 collective-permute-start.7
  118.0 6.7 %collective-permute-start.8 = (bf16[256,1152]{1,0:T(8,128)(2,1)}, bf16[256,1152]{1,0:T(8,128)(2,1)}, u32[]{:S(2)}, u32[]{:S(2)}) collective-permute-start(bf16[256,1152]{1,0:T(8,128)(2,1)} %get-tuple-element.26), channel_id=1, source_target_pairs={{32,0},{48,16},{64,32},{80,48},{96,64},{112,80},{128,96},{144,112}... | collective-permute-start | bytes 1769480 | tf_op jit(solution)/shard_map/ppermute | solution.py:153
  124.7 0.0 collective-permute-done.11
  124.7 0.0 copy-start.2
  124.7 9.4 %collective-permute-start.9 = (bf16[256,1152]{1,0:T(8,128)(2,1)S(1)}, bf16[256,1152]{1,0:T(8,128)(2,1)}, u32[]{:S(2)}, u32[]{:S(2)}) collective-permute-start(bf16[256,1152]{1,0:T(8,128)(2,1)S(1)} %get-tuple-element.27), channel_id=1, source_target_pairs={{448,0},{80,16},{480,32},{112,48},{0,64},{144,80},{32,96},{176,112... | collective-permute-start | bytes 1769480 | tf_op jit(solution)/shard_map/ppermute | solution.py:153
  134.1 0.0 copy-done.2
  134.1 0.6 reduce_sum.21
  134.7 0.7 reduce_sum.26
  135.5 0.1 reduce_sum.27
  135.6 0.8 tile.2
  136.4 29.5 %all-to-all-start = ((f32[512,1,128]{2,1,0:T(1,128)}), f32[512,1,128]{2,1,0:T(1,128)}, u32[]{:S(2)}, u32[]{:S(2)}) async-start(f32[512,1,128]{2,1,0:T(1,128)} %tile.2), calls=%async_computation | async-start | bytes 524288 | tf_op jit(solution)/shard_map/all_to_all | solution.py:159
  165.9 0.0 collective-permute-done.10
  165.9 2.0 %multiply_convert_fusion = bf16[256,1152]{1,0:T(8,128)(2,1)} fusion(f32[256,1152]{1,0:T(8,128)S(1)} %get-tuple-element.28, bf16[128,1152]{1,0:T(8,128)(2,1)} %copy-done.2, bf16[128,1152]{1,0:T(8,128)(2,1)} %collective-permute-done.10, f32[]{:T(128)} %bitcast), kind=kLoop, calls=%fused_computation | loop fusion | flops 2064384 | bytes 2359300 | tf_op jit(solution)/shard_map/convert_element_type | solution.py:169
  167.9 0.0 collective-permute-done.6
  167.9 0.0 collective-permute-done.7
  167.9 0.0 collective-permute-done.8
  168.0 0.0 collective-permute-done.9
  168.0 2.8 %multiply_convert_fusion.1 = bf16[256,1152]{1,0:T(8,128)(2,1)} fusion(bf16[256,1152]{1,0:T(8,128)(2,1)} %collective-permute-done.9, bf16[256,1152]{1,0:T(8,128)(2,1)} %collective-permute-done.8, bf16[256,1152]{1,0:T(8,128)(2,1)} %collective-permute-done.7, f32[256,1152]{1,0:T(8,128)S(1)} %get-tuple-element.23, bf16[256,1152]{1,0:T(8,128)(2,1)} %collective-permute-done.6, ...), kind=kLoop, calls=%fused_computation.1 | loop fusion | flops 2949120 | bytes 4128772 | tf_op jit(solution)/shard_map/convert_element_type | solution.py:168
  170.7 17.5 %all-to-all-done = f32[512,1,128]{2,1,0:T(1,128)} async-done(((f32[512,1,128]{2,1,0:T(1,128)}), f32[512,1,128]{2,1,0:T(1,128)}, u32[]{:S(2)}, u32[]{:S(2)}) %all-to-all-start) | async-done | bytes 262176 | tf_op jit(solution)/shard_map/all_to_all | solution.py:159
  188.2 1.0 reduce_sum.28
  189.3 0.6 fusion.1
  (1 shorter events, 0.0 us)
Async XLA Ops:
  0.6 51.8 %copy-start = (bf16[256,1152]{1,0:T(8,128)(2,1)S(1)}, bf16[256,1152]{1,0:T(8,128)(2,1)}, u32[]{:S(2)}) copy-start(bf16[256,1152]{1,0:T(8,128)(2,1)} %mine.5) | copy-start | bytes 1769476
  0.6 51.8 %copy-start.1 = (bf16[256,1152]{1,0:T(8,128)(2,1)S(1)}, bf16[256,1152]{1,0:T(8,128)(2,1)}, u32[]{:S(2)}) copy-start(bf16[256,1152]{1,0:T(8,128)(2,1)} %texts.3) | copy-start | bytes 1769476
  0.6 36.5 %collective-permute-start.3 = (bf16[256,1152]{1,0:T(8,128)(2,1)}, bf16[256,1152]{1,0:T(8,128)(2,1)S(1)}, u32[]{:S(2)}, u32[]{:S(2)}) collective-permute-start(bf16[256,1152]{1,0:T(8,128)(2,1)} %mine.5), channel_id=1, source_target_pairs={{448,0},{80,16},{480,32},{112,48},{0,64},{144,80},{32,96},{176,112... | collective-permute-start | bytes 1769480 | tf_op jit(solution)/shard_map/ppermute | solution.py:107
  6.4 44.9 %collective-permute-start.2 = (bf16[256,1152]{1,0:T(8,128)(2,1)}, bf16[256,1152]{1,0:T(8,128)(2,1)S(1)}, u32[]{:S(2)}, u32[]{:S(2)}) collective-permute-start(bf16[256,1152]{1,0:T(8,128)(2,1)} %mine.5), channel_id=1, source_target_pairs={{0,448},{16,80},{32,480},{48,112},{64,0},{80,144},{96,32},{112,176... | collective-permute-start | bytes 1769480 | tf_op jit(solution)/shard_map/ppermute | solution.py:107
  10.6 40.7 %collective-permute-start.1 = (bf16[256,1152]{1,0:T(8,128)(2,1)}, bf16[256,1152]{1,0:T(8,128)(2,1)S(1)}, u32[]{:S(2)}, u32[]{:S(2)}) collective-permute-start(bf16[256,1152]{1,0:T(8,128)(2,1)} %mine.5), channel_id=1, source_target_pairs={{0,32},{16,48},{32,64},{48,80},{64,96},{80,112},{96,128},{112,144}... | collective-permute-start | bytes 1769480 | tf_op jit(solution)/shard_map/ppermute | solution.py:107
  13.7 38.7 %collective-permute-start = (bf16[256,1152]{1,0:T(8,128)(2,1)}, bf16[256,1152]{1,0:T(8,128)(2,1)S(1)}, u32[]{:S(2)}, u32[]{:S(2)}) collective-permute-start(bf16[256,1152]{1,0:T(8,128)(2,1)} %mine.5), channel_id=1, source_target_pairs={{0,480},{16,496},{32,0},{48,16},{64,32},{80,48},{96,64},{112,80},{... | collective-permute-start | bytes 1769480 | tf_op jit(solution)/shard_map/ppermute | solution.py:107
  20.3 35.9 %collective-permute-start.4 = (bf16[128,1152]{1,0:T(8,128)(2,1)S(1)}, bf16[128,1152]{1,0:T(8,128)(2,1)S(1)}, u32[]{:S(2)}, u32[]{:S(2)}) collective-permute-start(bf16[128,1152]{1,0:T(8,128)(2,1)S(1)} %get-tuple-element.33), channel_id=1, source_target_pairs={{0,16},{16,0},{32,48},{48,32},{64,80},{80,64},{96,112},{112,96},{1... | collective-permute-start | bytes 884744 | tf_op jit(solution)/shard_map/ppermute | solution.py:104
  37.2 36.9 %collective-permute-start.5 = (bf16[128,1152]{1,0:T(8,128)(2,1)S(1)}, bf16[128,1152]{1,0:T(8,128)(2,1)S(1)}, u32[]{:S(2)}, u32[]{:S(2)}) collective-permute-start(bf16[128,1152]{1,0:T(8,128)(2,1)S(1)} %get-tuple-element.32), channel_id=1, source_target_pairs={{0,16},{16,0},{32,48},{48,32},{64,80},{80,64},{96,112},{112,96},{1... | collective-permute-start | bytes 884744 | tf_op jit(solution)/shard_map/ppermute | solution.py:104
  76.6 48.1 %collective-permute-start.11 = (bf16[128,1152]{1,0:T(8,128)(2,1)S(1)}, bf16[128,1152]{1,0:T(8,128)(2,1)S(1)}, u32[]{:S(2)}, u32[]{:S(2)}) collective-permute-start(bf16[128,1152]{1,0:T(8,128)(2,1)S(1)} %get-tuple-element.30), channel_id=1, source_target_pairs={{0,16},{16,0},{32,48},{48,32},{64,80},{80,64},{96,112},{112,96},{1... | collective-permute-start | bytes 884744 | tf_op jit(solution)/shard_map/ppermute | solution.py:141
  89.0 76.9 %collective-permute-start.10 = (bf16[128,1152]{1,0:T(8,128)(2,1)}, bf16[128,1152]{1,0:T(8,128)(2,1)}, u32[]{:S(2)}, u32[]{:S(2)}) collective-permute-start(bf16[128,1152]{1,0:T(8,128)(2,1)} %get-tuple-element.29), channel_id=1, source_target_pairs={{0,16},{16,0},{32,48},{48,32},{64,80},{80,64},{96,112},{112,96},{1... | collective-permute-start | bytes 884744 | tf_op jit(solution)/shard_map/ppermute | solution.py:141
  90.9 77.0 %collective-permute-start.6 = (bf16[256,1152]{1,0:T(8,128)(2,1)S(1)}, bf16[256,1152]{1,0:T(8,128)(2,1)}, u32[]{:S(2)}, u32[]{:S(2)}) collective-permute-start(bf16[256,1152]{1,0:T(8,128)(2,1)S(1)} %get-tuple-element.24), channel_id=1, source_target_pairs={{0,448},{16,80},{32,480},{48,112},{64,0},{80,144},{96,32},{112,176... | collective-permute-start | bytes 1769480 | tf_op jit(solution)/shard_map/ppermute | solution.py:123
  116.1 51.8 %collective-permute-start.7 = (bf16[256,1152]{1,0:T(8,128)(2,1)}, bf16[256,1152]{1,0:T(8,128)(2,1)}, u32[]{:S(2)}, u32[]{:S(2)}) collective-permute-start(bf16[256,1152]{1,0:T(8,128)(2,1)} %get-tuple-element.25), channel_id=1, source_target_pairs={{480,0},{496,16},{0,32},{16,48},{32,64},{48,80},{64,96},{80,112},{... | collective-permute-start | bytes 1769480 | tf_op jit(solution)/shard_map/ppermute | solution.py:153
  118.0 49.9 %collective-permute-start.8 = (bf16[256,1152]{1,0:T(8,128)(2,1)}, bf16[256,1152]{1,0:T(8,128)(2,1)}, u32[]{:S(2)}, u32[]{:S(2)}) collective-permute-start(bf16[256,1152]{1,0:T(8,128)(2,1)} %get-tuple-element.26), channel_id=1, source_target_pairs={{32,0},{48,16},{64,32},{80,48},{96,64},{112,80},{128,96},{144,112}... | collective-permute-start | bytes 1769480 | tf_op jit(solution)/shard_map/ppermute | solution.py:153
  124.7 9.4 %copy-start.2 = (bf16[128,1152]{1,0:T(8,128)(2,1)}, bf16[128,1152]{1,0:T(8,128)(2,1)S(1)}, u32[]{:S(2)}) copy-start(bf16[128,1152]{1,0:T(8,128)(2,1)S(1)} %collective-permute-done.11) | copy-start | bytes 884740
  124.7 43.2 %collective-permute-start.9 = (bf16[256,1152]{1,0:T(8,128)(2,1)S(1)}, bf16[256,1152]{1,0:T(8,128)(2,1)}, u32[]{:S(2)}, u32[]{:S(2)}) collective-permute-start(bf16[256,1152]{1,0:T(8,128)(2,1)S(1)} %get-tuple-element.27), channel_id=1, source_target_pairs={{448,0},{80,16},{480,32},{112,48},{0,64},{144,80},{32,96},{176,112... | collective-permute-start | bytes 1769480 | tf_op jit(solution)/shard_map/ppermute | solution.py:153
  136.4 51.8 %all-to-all-start = ((f32[512,1,128]{2,1,0:T(1,128)}), f32[512,1,128]{2,1,0:T(1,128)}, u32[]{:S(2)}, u32[]{:S(2)}) async-start(f32[512,1,128]{2,1,0:T(1,128)} %tile.2), calls=%async_computation | async-start | bytes 524288 | tf_op jit(solution)/shard_map/all_to_all | solution.py:159

commit v2 on v1

v2 whole, which is shorter than its diff:
```python
import jax
import jax.numpy as jnp
from jax import lax
from jax.experimental import pallas as pl
from jax.experimental.pallas import tpu as pltpu
from jax.sharding import Mesh
from jax.sharding import PartitionSpec as P

F32, BF16 = jnp.float32, jnp.bfloat16
VMEM = pl.BlockSpec(memory_space=pltpu.VMEM)
SMEM = pl.BlockSpec(memory_space=pltpu.SMEM)
PARAMS = pltpu.CompilerParams(vmem_limit_bytes=48 * 1024 * 1024)


def dot(left, right, left_dim, right_dim):
    return lax.dot_general(
        left, right, (((left_dim,), (right_dim,)), ((), ())), preferred_element_type=F32
    )


def fold(tile):
    return jnp.sum(tile.reshape(-1, 8, tile.shape[-1]), axis=0)


def score(scalars, texts, images, on_diagonal):
    products = dot(texts, images, 1, 1)
    slopes = jax.nn.sigmoid(scalars[0] * products + scalars[1])
    if on_diagonal:
        rows = lax.broadcasted_iota(jnp.int32, slopes.shape, 0)
        columns = lax.broadcasted_iota(jnp.int32, slopes.shape, 1)
        slopes = slopes - jnp.where(rows == columns, 1.0, 0.0)
    return slopes.astype(BF16), fold(slopes), fold(slopes * products)


def first_kernel(scalars, texts, mine, slopes_out, grad_out, sums_out, copy_out):
    half, bias_sum, scale_sum = score(scalars, texts[...], mine[...], True)
    slopes_out[...] = half
    grad_out[...] = dot(half, mine[...], 1, 0)
    copy_out[...] = mine[...]
    sums_out[0:8] = bias_sum
    sums_out[8:16] = scale_sum


def own_kernel(
    scalars, texts, ahead, behind, outer, inner, grad_in, sums_in, slopes_out, grad_out, inner_out, sums_out
):
    bias_sum, scale_sum, grad = sums_in[0:8], sums_in[8:16], grad_in[...]
    for slot, images in enumerate((ahead, behind, outer, inner)):
        half, bias_part, scale_part = score(scalars, texts[...], images[...], False)
        grad = grad + dot(half, images[...], 1, 0)
        bias_sum, scale_sum = bias_sum + bias_part, scale_sum + scale_part
        if slot == 3:
            inner_out[...] = dot(half, texts[...], 0, 0).astype(BF16)
        else:
            slopes_out[slot] = half
    grad_out[...] = grad
    sums_out[0:8] = bias_sum
    sums_out[8:16] = scale_sum


def lane_row(bias_sum, scale_sum):
    lane = lax.broadcasted_iota(jnp.int32, (1, 128), 1)
    return jnp.where(lane == 0, bias_sum, jnp.where(lane == 1, scale_sum, 0.0))


def far_kernel(scalars, texts, mine, ahead, behind, outer, sums, slopes_out, grad_out, row_out):
    bias_sum, scale_sum, grad = sums[0:8], sums[8:16], None
    for slot, images in enumerate((mine, ahead, behind, outer)):
        half, bias_part, scale_part = score(scalars, texts[...], images[...], False)
        part = dot(half, images[...], 1, 0)
        grad = part if grad is None else grad + part
        bias_sum, scale_sum = bias_sum + bias_part, scale_sum + scale_part
        slopes_out[slot] = half
    grad_out[...] = grad.astype(BF16)
    row_out[...] = jnp.broadcast_to(lane_row(jnp.sum(bias_sum), jnp.sum(scale_sum)), row_out.shape)


def images_kernel(
    texts, first_slopes, own_slopes, far_texts, far_slopes, rows, mine_out, ahead_out, behind_out, outer_out, row_out
):
    for slot, out in ((1, ahead_out), (2, behind_out), (3, outer_out), (0, mine_out)):
        own = first_slopes[...] if slot == 0 else own_slopes[slot - 1]
        grad = dot(own, texts[...], 0, 0) + dot(far_slopes[slot], far_texts[...], 0, 0)
        out[...] = grad.astype(out.dtype)
    row_out[...] = jnp.broadcast_to(jnp.sum(rows[...], axis=0, keepdims=True), row_out.shape)


def shape(rows, columns, kind):
    return jax.ShapeDtypeStruct((rows, columns), kind)


def cost(moved):
    return pl.CostEstimate(flops=0, bytes_accessed=moved, transcendentals=0)


def call(kernel, name, outs, in_smem, args, moved):
    return pl.pallas_call(
        kernel,
        out_shape=outs,
        in_specs=[SMEM] * in_smem + [VMEM] * (len(args) - in_smem),
        out_specs=(VMEM,) * len(outs),
        compiler_params=PARAMS,
        cost_estimate=pl.CostEstimate(flops=0, bytes_accessed=moved, transcendentals=0),
        name=name,
    )(*args)


def local(images, texts, log_temp, bias):
    rows, width = images.shape
    columns_count, halves = lax.axis_size(("x", "y")), lax.axis_size("half")
    in_column = halves * lax.axis_size("grp")
    stops = columns_count * halves
    scale = jnp.exp(log_temp[0])
    scalars = jnp.stack([scale, bias[0]])
    block = rows * width * 2

    def moved(value, pairs):
        return lax.ppermute(value, ("x", "y", "half"), pairs)

    def columns(count):
        return [(s, (s - 2 * count) % stops) for s in range(stops)]

    def back(pairs):
        return [(b, a) for a, b in pairs]

    flip = [(s, s ^ 1) for s in range(stops)]
    outward = [(s, (s - 4 * (1 - 2 * (s % 2))) % stops) for s in range(stops)]
    ways = (columns(1), columns(-1), outward, back(outward))

    far_texts = moved(texts, flip)
    first_slopes, text_first, sums, images_too = call(
        first_kernel,
        "first_pair",
        (shape(rows, rows, BF16), shape(rows, width, F32), shape(16, rows, F32), shape(rows, width, BF16)),
        1,
        (scalars, texts, images),
        100 * block,
    )
    near = [moved(images_too, way) for way in ways]
    far_texts, *near = lax.optimization_barrier((far_texts, *near))
    own_slopes, text_own, inner_part, sums = call(
        own_kernel,
        "own_pairs",
        (
            jax.ShapeDtypeStruct((3, rows, rows), BF16),
            shape(rows, width, F32),
            shape(rows, width, BF16),
            shape(16, rows, F32),
        ),
        1,
        (scalars, texts, *near, text_first, sums),
        block,
    )
    inner_back = moved(inner_part, back(ways[3]))
    far_slopes, far_grad, row_copies = call(
        far_kernel,
        "far_pairs",
        (
            jax.ShapeDtypeStruct((4, rows, rows), BF16),
            shape(rows, width, BF16),
            shape(columns_count, 128, F32),
        ),
        1,
        (scalars, far_texts, images, *near[:3], sums),
        block,
    )
    text_back = moved(far_grad, flip)
    level_rows = lax.all_to_all(row_copies, ("x", "y"), 0, 0, tiled=True)
    image_own, *image_parts, row_copies = call(
        images_kernel,
        "image_parts",
        (shape(rows, width, F32),) + (shape(rows, width, BF16),) * 3 + (shape(in_column, 128, F32),),
        0,
        (texts, first_slopes, own_slopes, far_texts, far_slopes, level_rows),
        block,
    )
    image_back = [moved(part, back(way)) for part, way in zip(image_parts, ways[:3], strict=True)]
    row_copies, text_back = lax.optimization_barrier((row_copies, text_back))
    sums_all = jnp.sum(lax.all_to_all(row_copies, ("half", "grp"), 0, 0, tiled=True), axis=0)

    batch_rows = rows * columns_count * in_column
    bias_grad = (sums_all[0] / batch_rows).reshape(1)
    temp_grad = (scale * sums_all[1] / batch_rows).reshape(1)
    image_sum = image_own + inner_back.astype(F32)
    for part in image_back:
        image_sum = image_sum + part.astype(F32)
    image_grad = (scale * image_sum).astype(BF16)
    text_grad = (scale * (text_own + text_back.astype(F32))).astype(BF16)
    return image_grad, text_grad, bias_grad, temp_grad


def solution(mesh):
    x_y_half = (4, 4, 2)
    fine = Mesh(mesh.devices.reshape(*x_y_half, -1), ("x", "y", "half", "grp"))
    split = P(("x", "y", "half", "grp"), None)
    return jax.shard_map(
        local, mesh=fine, in_specs=(split, split, P(), P()), out_specs=(split, split, P(), P()), check_vma=False
    )
```

time: 194 us -> 174 us (0.90); the launches traced: 193 us -> 171 us
  starting transfers between devices: 132 us -> 100 us
  waiting for transfers between devices: 33.3 us -> 39.9 us
  local copies, waits for them, and re-layouts: 3.27 us -> 8.72 us
  other arithmetic: 6.64 us -> 4.57 us
    ppermute x12 -> x10, starting transfers between devices: 103 us -> 60.2 us  [moved(): return lax.ppermute(value, ('x', 'y', 'half'), pairs)]
    ppermute x12 -> x10, waiting for transfers between devices: 15.8 us -> 32.6 us  [moved(): return lax.ppermute(value, ('x', 'y', 'half'), pairs)]
    all_to_all x1 -> x2, starting transfers between devices: 29.5 us -> 39.8 us  [the longest x1 34.2 us: local(): lax.all_to_all(row_copies, ('half', 'grp'), 0, 0, tiled=True)]
    all_to_all x1 -> x2, waiting for transfers between devices: 17.5 us -> 7.31 us  [the longest x1 7.31 us: local(): lax.all_to_all(row_copies, ('half', 'grp'), 0, 0, tiled=True)]
    unnamed x6 -> x26, local copies, waits for them, and re-layouts: 0.01 us -> 8.14 us
  transfers between devices with their start and end apart: 13 -> 12, of which waited for: 3 -> 4; matrix products, arithmetic and copies ran while one was open for 4% -> 3% of each run, Pallas kernels for 5% -> 2%
where the time goes in v2:
time: 174 us; the launch traced here: 171 us
  starting transfers between devices  100 us (57%)
  waiting for transfers between devices  39.9 us (23%)
  Pallas kernels  11.6 us (7%)
  local copies, waits for them, and re-layouts  8.72 us (5%)
  between operations  5.72 us (3%)
  other arithmetic  4.57 us (3%)
    ppermute x10, starting transfers between devices, moved(): return lax.ppermute(value, ('x', 'y', 'half'), pairs)  60.2 us
    all_to_all x1, starting transfers between devices, local(): lax.all_to_all(row_copies, ('half', 'grp'), 0, 0, tiled=True)  34.2 us
    ppermute x10, waiting for transfers between devices, moved(): return lax.ppermute(value, ('x', 'y', 'half'), pairs)  32.6 us
    pallas_call x4, Pallas kernels, call(): pl.pallas_call(kernel, out_shape=outs, in_specs=[SMEM] * in_smem + [VMEM]...  11.6 us
    unnamed x26, local copies, waits for them, and re-layouts  8.14 us
    all_to_all x1, waiting for transfers between devices, local(): lax.all_to_all(row_copies, ('half', 'grp'), 0, 0, tiled=True)  7.31 us
    all_to_all x1, starting transfers between devices, local(): level_rows = lax.all_to_all(row_copies, ('x', 'y'), 0, 0, tiled=True)  5.57 us
  transfers between devices with their start and end apart: 12, of which 4 were waited for; matrix products, arithmetic and copies ran while one was open for 3% of the time, Pallas kernels for 2%

profile of v2, /device:TPU:1, one launch (start us, length us, event | category | flops | bytes accessed | tf_op | source)
XLA Modules:
  0.0 170.6 jit_solution(1271405444196002801)
XLA Ops:
  0.6 16.3 %collective-permute-start = (bf16[256,1152]{1,0:T(8,128)(2,1)}, bf16[256,1152]{1,0:T(8,128)(2,1)S(1)}, u32[]{:S(2)}, u32[]{:S(2)}) collective-permute-start(bf16[256,1152]{1,0:T(8,128)(2,1)} %texts.5), channel_id=1, source_target_pairs={{0,16},{16,0},{32,48},{48,32},{64,80},{80,64},{96,112},{112,96},{1... | collective-permute-start | bytes 1769480 | tf_op jit(solution)/shard_map/ppermute | solution.py:118
  18.2 0.1 pad_maximum_fusion.scalars
  18.3 0.0 copy-start
  18.3 1.1 copy-done
  19.4 0.0 copy-start.2
  19.4 1.1 copy-done.2
  20.4 1.5 first_pair.1
  21.9 0.0 copy-start.4
  21.9 1.0 copy-done.4
  23.0 0.0 copy-start.9
  23.0 0.6 copy-done.9
  23.6 4.8 %collective-permute-start.4 = (bf16[256,1152]{1,0:T(8,128)(2,1)S(1)}, bf16[256,1152]{1,0:T(8,128)(2,1)S(1)}, u32[]{:S(2)}, u32[]{:S(2)}) collective-permute-start(bf16[256,1152]{1,0:T(8,128)(2,1)S(1)} %get-tuple-element.28), channel_id=1, source_target_pairs={{448,0},{80,16},{480,32},{112,48},{0,64},{144,80},{32,96},{176,112... | collective-permute-start | bytes 1769480 | tf_op jit(solution)/shard_map/ppermute | solution.py:118
  28.4 4.1 %collective-permute-start.3 = (bf16[256,1152]{1,0:T(8,128)(2,1)S(1)}, bf16[256,1152]{1,0:T(8,128)(2,1)S(1)}, u32[]{:S(2)}, u32[]{:S(2)}) collective-permute-start(bf16[256,1152]{1,0:T(8,128)(2,1)S(1)} %get-tuple-element.28), channel_id=1, source_target_pairs={{0,448},{16,80},{32,480},{48,112},{64,0},{80,144},{96,32},{112,176... | collective-permute-start | bytes 1769480 | tf_op jit(solution)/shard_map/ppermute | solution.py:118
  32.5 3.2 %collective-permute-start.2 = (bf16[256,1152]{1,0:T(8,128)(2,1)S(1)}, bf16[256,1152]{1,0:T(8,128)(2,1)S(1)}, u32[]{:S(2)}, u32[]{:S(2)}) collective-permute-start(bf16[256,1152]{1,0:T(8,128)(2,1)S(1)} %get-tuple-element.28), channel_id=1, source_target_pairs={{0,32},{16,48},{32,64},{48,80},{64,96},{80,112},{96,128},{112,144}... | collective-permute-start | bytes 1769480 | tf_op jit(solution)/shard_map/ppermute | solution.py:118
  35.7 5.4 %collective-permute-start.1 = (bf16[256,1152]{1,0:T(8,128)(2,1)S(1)}, bf16[256,1152]{1,0:T(8,128)(2,1)S(1)}, u32[]{:S(2)}, u32[]{:S(2)}) collective-permute-start(bf16[256,1152]{1,0:T(8,128)(2,1)S(1)} %get-tuple-element.28), channel_id=1, source_target_pairs={{0,480},{16,496},{32,0},{48,16},{64,32},{80,48},{96,64},{112,80},{... | collective-permute-start | bytes 1769480 | tf_op jit(solution)/shard_map/ppermute | solution.py:118
  41.2 0.0 collective-permute-done.texts.far_texts
  41.2 11.6 %collective-permute-done.4.inner = bf16[256,1152]{1,0:T(8,128)(2,1)S(1)} collective-permute-done((bf16[256,1152]{1,0:T(8,128)(2,1)S(1)}, bf16[256,1152]{1,0:T(8,128)(2,1)S(1)}, u32[]{:S(2)}, u32[]{:S(2)}) %collective-permute-start.4) | collective-permute-done | bytes 589856 | tf_op jit(solution)/shard_map/ppermute | solution.py:118
  52.8 16.9 %collective-permute-done.3.outer = bf16[256,1152]{1,0:T(8,128)(2,1)S(1)} collective-permute-done((bf16[256,1152]{1,0:T(8,128)(2,1)S(1)}, bf16[256,1152]{1,0:T(8,128)(2,1)S(1)}, u32[]{:S(2)}, u32[]{:S(2)}) %collective-permute-start.3) | collective-permute-done | bytes 589856 | tf_op jit(solution)/shard_map/ppermute | solution.py:118
  69.6 0.0 collective-permute-done.2.behind
  69.6 4.1 %collective-permute-done.1.ahead = bf16[256,1152]{1,0:T(8,128)(2,1)S(1)} collective-permute-done((bf16[256,1152]{1,0:T(8,128)(2,1)S(1)}, bf16[256,1152]{1,0:T(8,128)(2,1)S(1)}, u32[]{:S(2)}, u32[]{:S(2)}) %collective-permute-start.1) | collective-permute-done | bytes 589856 | tf_op jit(solution)/shard_map/ppermute | solution.py:118
  73.8 0.0 copy-start.3
  73.8 4.1 %own_pairs.1 = (bf16[3,256,256]{2,1,0:T(8,128)(2,1)S(1)}, f32[256,1152]{1,0:T(8,128)S(1)}, bf16[256,1152]{1,0:T(8,128)(2,1)S(1)}, f32[16,256]{1,0:T(8,128)S(1)}) custom-call(f32[2]{0:T(128)S(1)} %pad_maximum_fusion.scalars, bf16[256,1152]{1,0:T(8,128)(2,1)S(1)} %copy-done, bf16[256,1152]{1,0:T(8,128)(2,1)S(1)} %collective-permute-done.1.ahead, ...), custom_call_target="tpu_custom_call" | custom-call | bytes 589824 | tf_op jit(solution)/shard_map/own_pairs/pallas_call | solution.py:97
  77.8 0.0 copy-start.7
  77.8 0.0 copy-start.12
  77.9 0.0 copy-done.3
  77.9 0.0 copy-start.1
  77.9 3.7 %far_pairs.1 = (bf16[4,256,256]{2,1,0:T(8,128)(2,1)S(1)}, bf16[256,1152]{1,0:T(8,128)(2,1)}, f32[16,128]{1,0:T(8,128)}) custom-call(f32[2]{0:T(128)S(1)} %pad_maximum_fusion.scalars, bf16[256,1152]{1,0:T(8,128)(2,1)S(1)} %collective-permute-done.texts.far_texts, bf16[256,1152]{1,0:T(8,128)(2,1)S(1)} %copy-done.3, ...), custom_call_target="tpu_custom_call" | custom-call | bytes 589824 | tf_op jit(solution)/shard_map/far_pairs/pallas_call | solution.py:97
  81.6 0.0 copy-done.7
  81.6 0.0 copy-done.12
  81.6 0.0 copy-start.5
  81.6 0.8 copy-done.5
  82.4 9.0 %collective-permute-start.9 = (bf16[256,1152]{1,0:T(8,128)(2,1)}, bf16[256,1152]{1,0:T(8,128)(2,1)}, u32[]{:S(2)}, u32[]{:S(2)}) collective-permute-start(bf16[256,1152]{1,0:T(8,128)(2,1)} %get-tuple-element.47), channel_id=1, source_target_pairs={{0,16},{16,0},{32,48},{48,32},{64,80},{80,64},{96,112},{112,96},{1... | collective-permute-start | bytes 1769480 | tf_op jit(solution)/shard_map/ppermute | solution.py:118
  91.4 5.6 %all-to-all-start = ((f32[16,1,128]{2,1,0:T(1,128)}), f32[16,1,128]{2,1,0:T(1,128)S(1)}, u32[]{:S(2)}, u32[]{:S(2)}) async-start(f32[16,1,128]{2,1,0:T(1,128)} %bitcast.2), calls=%async_computation | async-start | bytes 16384 | tf_op jit(solution)/shard_map/all_to_all | solution.py:168
  97.0 6.9 %collective-permute-start.5 = (bf16[256,1152]{1,0:T(8,128)(2,1)}, bf16[256,1152]{1,0:T(8,128)(2,1)}, u32[]{:S(2)}, u32[]{:S(2)}) collective-permute-start(bf16[256,1152]{1,0:T(8,128)(2,1)} %copy-done.12), channel_id=1, source_target_pairs={{0,448},{16,80},{32,480},{48,112},{64,0},{80,144},{96,32},{112,176... | collective-permute-start | bytes 1769480 | tf_op jit(solution)/shard_map/ppermute | solution.py:118
  103.9 0.0 all-to-all-done
  103.9 0.0 copy-done.1
  103.9 0.0 copy-start.6
  103.9 1.0 copy-done.6
  104.9 0.0 copy-start.8
  104.9 1.0 copy-done.8
  105.9 0.0 copy-start.10
  105.9 0.9 copy-done.10
  106.8 2.4 %image_parts.1 = (f32[256,1152]{1,0:T(8,128)S(1)}, bf16[256,1152]{1,0:T(8,128)(2,1)}, bf16[256,1152]{1,0:T(8,128)(2,1)}, bf16[256,1152]{1,0:T(8,128)(2,1)}, f32[32,128]{1,0:T(8,128)S(1)}) custom-call(bf16[256,1152]{1,0:T(8,128)(2,1)S(1)} %copy-done.1, bf16[256,256]{1,0:T(8,128)(2,1)S(1)} %copy-done.10, bf16[3,256,256]{2,1,0:T(8,128)(2,1)S(1)} %copy-done.8, ...), custom_call_target="tpu_custom_call" | custom-call | bytes 589824 | tf_op jit(solution)/shard_map/image_parts/pallas_call | solution.py:97
  109.2 0.0 copy-start.11
  109.2 0.6 copy-done.11
  109.8 2.2 %collective-permute-start.6 = (bf16[256,1152]{1,0:T(8,128)(2,1)}, bf16[256,1152]{1,0:T(8,128)(2,1)S(1)}, u32[]{:S(2)}, u32[]{:S(2)}) collective-permute-start(bf16[256,1152]{1,0:T(8,128)(2,1)} %get-tuple-element.42), channel_id=1, source_target_pairs={{480,0},{496,16},{0,32},{16,48},{32,64},{48,80},{64,96},{80,112},{... | collective-permute-start | bytes 1769480 | tf_op jit(solution)/shard_map/ppermute | solution.py:118
  112.0 6.4 %collective-permute-start.7 = (bf16[256,1152]{1,0:T(8,128)(2,1)}, bf16[256,1152]{1,0:T(8,128)(2,1)S(1)}, u32[]{:S(2)}, u32[]{:S(2)}) collective-permute-start(bf16[256,1152]{1,0:T(8,128)(2,1)} %get-tuple-element.43), channel_id=1, source_target_pairs={{32,0},{48,16},{64,32},{80,48},{96,64},{112,80},{128,96},{144,112}... | collective-permute-start | bytes 1769480 | tf_op jit(solution)/shard_map/ppermute | solution.py:118
  118.4 1.9 %collective-permute-start.8 = (bf16[256,1152]{1,0:T(8,128)(2,1)}, bf16[256,1152]{1,0:T(8,128)(2,1)}, u32[]{:S(2)}, u32[]{:S(2)}) collective-permute-start(bf16[256,1152]{1,0:T(8,128)(2,1)} %get-tuple-element.44), channel_id=1, source_target_pairs={{448,0},{80,16},{480,32},{112,48},{0,64},{144,80},{32,96},{176,112... | collective-permute-start | bytes 1769480 | tf_op jit(solution)/shard_map/ppermute | solution.py:118
  120.4 0.0 collective-permute-done.9
  120.4 34.2 %all-to-all-start.1 = ((f32[32,1,128]{2,1,0:T(1,128)}), f32[32,1,128]{2,1,0:T(1,128)S(1)}, u32[]{:S(2)}, u32[]{:S(2)}) async-start(f32[32,1,128]{2,1,0:T(1,128)} %bitcast.11), calls=%async_computation.1 | async-start | bytes 32768 | tf_op jit(solution)/shard_map/all_to_all | solution.py:179
  154.6 2.0 %multiply_convert_fusion = bf16[256,1152]{1,0:T(8,128)(2,1)} fusion(f32[256,1152]{1,0:T(8,128)S(1)} %get-tuple-element.45, bf16[256,1152]{1,0:T(8,128)(2,1)} %collective-permute-done.9, f32[]{:T(128)} %bitcast), kind=kLoop, calls=%fused_computation | loop fusion | flops 1179648 | bytes 2359300 | tf_op jit(solution)/shard_map/convert_element_type | solution.py:188
  156.6 0.0 collective-permute-done.5
  156.6 0.0 collective-permute-done.6
  156.6 0.0 collective-permute-done.7
  156.6 0.0 collective-permute-done.8
  156.7 2.4 %multiply_convert_fusion.1 = bf16[256,1152]{1,0:T(8,128)(2,1)} fusion(bf16[256,1152]{1,0:T(8,128)(2,1)} %collective-permute-done.8, bf16[256,1152]{1,0:T(8,128)(2,1)S(1)} %collective-permute-done.7, bf16[256,1152]{1,0:T(8,128)(2,1)S(1)} %collective-permute-done.6, f32[256,1152]{1,0:T(8,128)S(1)} %get-tuple-element.40, ...), kind=kLoop, calls=%fused_computation.1 | loop fusion | flops 2949120 | bytes 4128772 | tf_op jit(solution)/shard_map/convert_element_type | solution.py:187
  159.1 7.3 %all-to-all-done.1 = f32[32,1,128]{2,1,0:T(1,128)S(1)} async-done(((f32[32,1,128]{2,1,0:T(1,128)}), f32[32,1,128]{2,1,0:T(1,128)S(1)}, u32[]{:S(2)}, u32[]{:S(2)}) %all-to-all-start.1) | async-done | bytes 16416 | tf_op jit(solution)/shard_map/all_to_all | solution.py:179
  166.4 0.1 reduce_sum.9
  166.4 0.6 fusion
Async XLA Ops:
  0.6 40.5 %collective-permute-start = (bf16[256,1152]{1,0:T(8,128)(2,1)}, bf16[256,1152]{1,0:T(8,128)(2,1)S(1)}, u32[]{:S(2)}, u32[]{:S(2)}) collective-permute-start(bf16[256,1152]{1,0:T(8,128)(2,1)} %texts.5), channel_id=1, source_target_pairs={{0,16},{16,0},{32,48},{48,32},{64,80},{80,64},{96,112},{112,96},{1... | collective-permute-start | bytes 1769480 | tf_op jit(solution)/shard_map/ppermute | solution.py:118
  18.3 1.1 copy-start
  19.4 1.1 copy-start.2
  21.9 1.0 copy-start.4
  23.0 0.6 copy-start.9
  23.6 29.2 %collective-permute-start.4 = (bf16[256,1152]{1,0:T(8,128)(2,1)S(1)}, bf16[256,1152]{1,0:T(8,128)(2,1)S(1)}, u32[]{:S(2)}, u32[]{:S(2)}) collective-permute-start(bf16[256,1152]{1,0:T(8,128)(2,1)S(1)} %get-tuple-element.28), channel_id=1, source_target_pairs={{448,0},{80,16},{480,32},{112,48},{0,64},{144,80},{32,96},{176,112... | collective-permute-start | bytes 1769480 | tf_op jit(solution)/shard_map/ppermute | solution.py:118
  28.4 41.2 %collective-permute-start.3 = (bf16[256,1152]{1,0:T(8,128)(2,1)S(1)}, bf16[256,1152]{1,0:T(8,128)(2,1)S(1)}, u32[]{:S(2)}, u32[]{:S(2)}) collective-permute-start(bf16[256,1152]{1,0:T(8,128)(2,1)S(1)} %get-tuple-element.28), channel_id=1, source_target_pairs={{0,448},{16,80},{32,480},{48,112},{64,0},{80,144},{96,32},{112,176... | collective-permute-start | bytes 1769480 | tf_op jit(solution)/shard_map/ppermute | solution.py:118
  32.5 37.1 %collective-permute-start.2 = (bf16[256,1152]{1,0:T(8,128)(2,1)S(1)}, bf16[256,1152]{1,0:T(8,128)(2,1)S(1)}, u32[]{:S(2)}, u32[]{:S(2)}) collective-permute-start(bf16[256,1152]{1,0:T(8,128)(2,1)S(1)} %get-tuple-element.28), channel_id=1, source_target_pairs={{0,32},{16,48},{32,64},{48,80},{64,96},{80,112},{96,128},{112,144}... | collective-permute-start | bytes 1769480 | tf_op jit(solution)/shard_map/ppermute | solution.py:118
  35.7 38.1 %collective-permute-start.1 = (bf16[256,1152]{1,0:T(8,128)(2,1)S(1)}, bf16[256,1152]{1,0:T(8,128)(2,1)S(1)}, u32[]{:S(2)}, u32[]{:S(2)}) collective-permute-start(bf16[256,1152]{1,0:T(8,128)(2,1)S(1)} %get-tuple-element.28), channel_id=1, source_target_pairs={{0,480},{16,496},{32,0},{48,16},{64,32},{80,48},{96,64},{112,80},{... | collective-permute-start | bytes 1769480 | tf_op jit(solution)/shard_map/ppermute | solution.py:118
  73.8 4.1 %copy-start.3 = (bf16[256,1152]{1,0:T(8,128)(2,1)S(1)}, bf16[256,1152]{1,0:T(8,128)(2,1)}, u32[]{:S(2)}) copy-start(bf16[256,1152]{1,0:T(8,128)(2,1)} %mine.3) | copy-start | bytes 1769476
  77.8 3.8 %copy-start.7 = (bf16[3,256,256]{2,1,0:T(8,128)(2,1)}, bf16[3,256,256]{2,1,0:T(8,128)(2,1)S(1)}, u32[]{:S(2)}) copy-start(bf16[3,256,256]{2,1,0:T(8,128)(2,1)S(1)} %get-tuple-element.35.own_slopes) | copy-start | bytes 1179652
  77.8 3.8 %copy-start.12 = (bf16[256,1152]{1,0:T(8,128)(2,1)}, bf16[256,1152]{1,0:T(8,128)(2,1)S(1)}, u32[]{:S(2)}) copy-start(bf16[256,1152]{1,0:T(8,128)(2,1)S(1)} %get-tuple-element.41) | copy-start | bytes 1769476
  77.9 26.0 %copy-start.1 = (bf16[256,1152]{1,0:T(8,128)(2,1)S(1)}, bf16[256,1152]{1,0:T(8,128)(2,1)}, u32[]{:S(2)}) copy-start(bf16[256,1152]{1,0:T(8,128)(2,1)} %texts.5) | copy-start | bytes 1769476
  81.6 0.8 copy-start.5
  82.4 38.0 %collective-permute-start.9 = (bf16[256,1152]{1,0:T(8,128)(2,1)}, bf16[256,1152]{1,0:T(8,128)(2,1)}, u32[]{:S(2)}, u32[]{:S(2)}) collective-permute-start(bf16[256,1152]{1,0:T(8,128)(2,1)} %get-tuple-element.47), channel_id=1, source_target_pairs={{0,16},{16,0},{32,48},{48,32},{64,80},{80,64},{96,112},{112,96},{1... | collective-permute-start | bytes 1769480 | tf_op jit(solution)/shard_map/ppermute | solution.py:118
  91.4 12.5 %all-to-all-start = ((f32[16,1,128]{2,1,0:T(1,128)}), f32[16,1,128]{2,1,0:T(1,128)S(1)}, u32[]{:S(2)}, u32[]{:S(2)}) async-start(f32[16,1,128]{2,1,0:T(1,128)} %bitcast.2), calls=%async_computation | async-start | bytes 16384 | tf_op jit(solution)/shard_map/all_to_all | solution.py:168
  97.0 59.6 %collective-permute-start.5 = (bf16[256,1152]{1,0:T(8,128)(2,1)}, bf16[256,1152]{1,0:T(8,128)(2,1)}, u32[]{:S(2)}, u32[]{:S(2)}) collective-permute-start(bf16[256,1152]{1,0:T(8,128)(2,1)} %copy-done.12), channel_id=1, source_target_pairs={{0,448},{16,80},{32,480},{48,112},{64,0},{80,144},{96,32},{112,176... | collective-permute-start | bytes 1769480 | tf_op jit(solution)/shard_map/ppermute | solution.py:118
  103.9 1.0 copy-start.6
  104.9 1.0 copy-start.8
  105.9 0.9 copy-start.10
  109.2 0.6 copy-start.11
  109.8 46.8 %collective-permute-start.6 = (bf16[256,1152]{1,0:T(8,128)(2,1)}, bf16[256,1152]{1,0:T(8,128)(2,1)S(1)}, u32[]{:S(2)}, u32[]{:S(2)}) collective-permute-start(bf16[256,1152]{1,0:T(8,128)(2,1)} %get-tuple-element.42), channel_id=1, source_target_pairs={{480,0},{496,16},{0,32},{16,48},{32,64},{48,80},{64,96},{80,112},{... | collective-permute-start | bytes 1769480 | tf_op jit(solution)/shard_map/ppermute | solution.py:118
  112.0 44.6 %collective-permute-start.7 = (bf16[256,1152]{1,0:T(8,128)(2,1)}, bf16[256,1152]{1,0:T(8,128)(2,1)S(1)}, u32[]{:S(2)}, u32[]{:S(2)}) collective-permute-start(bf16[256,1152]{1,0:T(8,128)(2,1)} %get-tuple-element.43), channel_id=1, source_target_pairs={{32,0},{48,16},{64,32},{80,48},{96,64},{112,80},{128,96},{144,112}... | collective-permute-start | bytes 1769480 | tf_op jit(solution)/shard_map/ppermute | solution.py:118
  118.4 38.2 %collective-permute-start.8 = (bf16[256,1152]{1,0:T(8,128)(2,1)}, bf16[256,1152]{1,0:T(8,128)(2,1)}, u32[]{:S(2)}, u32[]{:S(2)}) collective-permute-start(bf16[256,1152]{1,0:T(8,128)(2,1)} %get-tuple-element.44), channel_id=1, source_target_pairs={{448,0},{80,16},{480,32},{112,48},{0,64},{144,80},{32,96},{176,112... | collective-permute-start | bytes 1769480 | tf_op jit(solution)/shard_map/ppermute | solution.py:118
  120.4 46.0 %all-to-all-start.1 = ((f32[32,1,128]{2,1,0:T(1,128)}), f32[32,1,128]{2,1,0:T(1,128)S(1)}, u32[]{:S(2)}, u32[]{:S(2)}) async-start(f32[32,1,128]{2,1,0:T(1,128)} %bitcast.11), calls=%async_computation.1 | async-start | bytes 32768 | tf_op jit(solution)/shard_map/all_to_all | solution.py:179

commit v3 on v2

v3 whole, which is shorter than its diff:
```python
import jax
import jax.numpy as jnp
from jax import lax
from jax.experimental import pallas as pl
from jax.experimental.pallas import tpu as pltpu
from jax.sharding import Mesh
from jax.sharding import PartitionSpec as P

F32, BF16 = jnp.float32, jnp.bfloat16
VMEM = pl.BlockSpec(memory_space=pltpu.VMEM)
SMEM = pl.BlockSpec(memory_space=pltpu.SMEM)
PARAMS = pltpu.CompilerParams(vmem_limit_bytes=48 * 1024 * 1024)


def dot(left, right, left_dim, right_dim):
    return lax.dot_general(
        left, right, (((left_dim,), (right_dim,)), ((), ())), preferred_element_type=F32
    )


def fold(tile):
    return jnp.sum(tile.reshape(-1, 8, tile.shape[-1]), axis=0)


def score(scalars, texts, images, on_diagonal):
    products = dot(texts, images, 1, 1)
    slopes = jax.nn.sigmoid(scalars[0] * products + scalars[1])
    if on_diagonal:
        rows = lax.broadcasted_iota(jnp.int32, slopes.shape, 0)
        columns = lax.broadcasted_iota(jnp.int32, slopes.shape, 1)
        slopes = slopes - jnp.where(rows == columns, 1.0, 0.0)
    return slopes.astype(BF16), fold(slopes), fold(slopes * products)


def first_kernel(scalars, texts, mine, slopes_out, grad_out, sums_out):
    half, bias_sum, scale_sum = score(scalars, texts[...], mine[...], True)
    slopes_out[...] = half
    grad_out[...] = dot(half, mine[...], 1, 0)
    sums_out[0:8] = bias_sum
    sums_out[8:16] = scale_sum


def own_kernel(scalars, texts, *refs):
    images, (grad_in, sums_in, slopes_out, grad_out, row_out) = refs[:4], refs[4:]
    bias_sum, scale_sum, grad = sums_in[0:8], sums_in[8:16], grad_in[...]
    for slot, near in enumerate(images):
        half, bias_part, scale_part = score(scalars, texts[...], near[...], False)
        grad = grad + dot(half, near[...], 1, 0)
        bias_sum, scale_sum = bias_sum + bias_part, scale_sum + scale_part
        slopes_out[slot] = half
    grad_out[...] = grad
    row_out[...] = jnp.broadcast_to(lane_row(jnp.sum(bias_sum), jnp.sum(scale_sum)), row_out.shape)


def lane_row(bias_sum, scale_sum):
    lane = lax.broadcasted_iota(jnp.int32, (1, 128), 1)
    return jnp.where(lane == 0, bias_sum, jnp.where(lane == 1, scale_sum, 0.0))


def far_kernel(scalars, texts, mine, ahead, behind, ahead_2, behind_2, sums, slopes_out, grad_out, sums_out):
    bias_sum, scale_sum, grad = sums[0:8], sums[8:16], None
    outer = jnp.where(scalars[2] > 0.5, ahead_2[...], behind_2[...])
    for slot, images in enumerate((mine[...], ahead[...], behind[...], outer)):
        half, bias_part, scale_part = score(scalars, texts[...], images, False)
        part = dot(half, images, 1, 0)
        grad = part if grad is None else grad + part
        bias_sum, scale_sum = bias_sum + bias_part, scale_sum + scale_part
        if slot < 3:
            slopes_out[slot] = half
        else:
            slopes_out[3] = jnp.where(scalars[2] > 0.5, half, jnp.zeros_like(half))
            slopes_out[4] = jnp.where(scalars[2] > 0.5, jnp.zeros_like(half), half)
    grad_out[...] = grad.astype(BF16)
    sums_out[0:8] = bias_sum
    sums_out[8:16] = scale_sum


def images_kernel(texts, first_slopes, own_slopes, far_texts, far_slopes, rows, *outs):
    for slot in (3, 4, 1, 2, 0):
        own = first_slopes[...] if slot == 0 else own_slopes[slot - 1]
        grad = dot(own, texts[...], 0, 0) + dot(far_slopes[slot], far_texts[...], 0, 0)
        outs[slot][...] = grad.astype(outs[slot].dtype)
    outs[5][...] = jnp.broadcast_to(jnp.sum(rows[...], axis=0, keepdims=True), outs[5].shape)


def shape(rows, columns, kind):
    return jax.ShapeDtypeStruct((rows, columns), kind)


def cost(moved):
    return pl.CostEstimate(flops=0, bytes_accessed=moved, transcendentals=0)


def call(kernel, name, outs, in_smem, args, moved):
    return pl.pallas_call(
        kernel,
        out_shape=outs,
        in_specs=[SMEM] * in_smem + [VMEM] * (len(args) - in_smem),
        out_specs=(VMEM,) * len(outs),
        compiler_params=PARAMS,
        cost_estimate=pl.CostEstimate(flops=0, bytes_accessed=moved, transcendentals=0),
        name=name,
    )(*args)


def local(images, texts, log_temp, bias):
    rows, width = images.shape
    columns_count, halves = lax.axis_size(("x", "y")), lax.axis_size("half")
    in_column = halves * lax.axis_size("grp")
    stops = columns_count * halves
    scale = jnp.exp(log_temp[0])
    first_half = (lax.axis_index("half") == 0).astype(F32)
    scalars = jnp.stack([scale, bias[0], first_half])
    block = rows * width * 2

    def moved(value, pairs):
        return lax.ppermute(value, ("x", "y", "half"), pairs)

    def columns(count):
        return [(s, (s - 2 * count) % stops) for s in range(stops)]

    def back(pairs):
        return [(b, a) for a, b in pairs]

    flip = [(s, s ^ 1) for s in range(stops)]
    ways = (columns(1), columns(-1), columns(2), columns(-2))

    far_texts = moved(texts, flip)
    ahead, behind = moved(images, ways[0]), moved(images, ways[1])
    ahead_2, behind_2 = moved(images, ways[2]), moved(images, ways[3])
    first_slopes, text_first, sums = call(
        first_kernel,
        "first_pair",
        (shape(rows, rows, BF16), shape(rows, width, F32), shape(16, rows, F32)),
        1,
        (scalars, texts, images),
        100 * block,
    )
    far_texts, ahead, behind, ahead_2, behind_2 = lax.optimization_barrier(
        (far_texts, ahead, behind, ahead_2, behind_2)
    )
    near = (ahead, behind, ahead_2, behind_2)
    far_slopes, far_grad, sums = call(
        far_kernel,
        "far_pairs",
        (jax.ShapeDtypeStruct((5, rows, rows), BF16), shape(rows, width, BF16), shape(16, rows, F32)),
        1,
        (scalars, far_texts, images, *near, sums),
        block,
    )
    text_back = moved(far_grad, flip)
    own_slopes, text_own, row_copies = call(
        own_kernel,
        "own_pairs",
        (
            jax.ShapeDtypeStruct((4, rows, rows), BF16),
            shape(rows, width, F32),
            shape(columns_count, 128, F32),
        ),
        1,
        (scalars, texts, *near, text_first, sums),
        block,
    )
    level_rows = lax.all_to_all(row_copies, ("x", "y"), 0, 0, tiled=True)
    image_own, *image_parts, row_copies = call(
        images_kernel,
        "image_parts",
        (shape(rows, width, F32),) + (shape(rows, width, BF16),) * 4 + (shape(in_column, 128, F32),),
        0,
        (texts, first_slopes, own_slopes, far_texts, far_slopes, level_rows),
        block,
    )
    image_back = [moved(part, back(way)) for part, way in zip(image_parts, ways, strict=True)]
    row_copies, text_back = lax.optimization_barrier((row_copies, text_back))
    sums_all = jnp.sum(lax.all_to_all(row_copies, ("half", "grp"), 0, 0, tiled=True), axis=0)

    batch_rows = rows * columns_count * in_column
    bias_grad = (sums_all[0] / batch_rows).reshape(1)
    temp_grad = (scale * sums_all[1] / batch_rows).reshape(1)
    image_sum = image_own
    for part in image_back:
        image_sum = image_sum + part.astype(F32)
    image_grad = (scale * image_sum).astype(BF16)
    text_grad = (scale * (text_own + text_back.astype(F32))).astype(BF16)
    return image_grad, text_grad, bias_grad, temp_grad


def solution(mesh):
    x_y_half = (4, 4, 2)
    fine = Mesh(mesh.devices.reshape(*x_y_half, -1), ("x", "y", "half", "grp"))
    split = P(("x", "y", "half", "grp"), None)
    return jax.shard_map(
        local, mesh=fine, in_specs=(split, split, P(), P()), out_specs=(split, split, P(), P()), check_vma=False
    )
```

time: 174 us -> 160 us (0.920)
  the two profiles are of different devices: /device:TPU:1 before, /device:TPU:62 now
where the time goes in v3:
time: 160 us; the launch traced here: 159 us
  starting transfers between devices  67.8 us (42%)
  waiting for transfers between devices  54.7 us (34%)
  blocking collectives  11 us (7%)
  Pallas kernels  10.5 us (7%)
  between operations  5.65 us (4%)
  other arithmetic  4.75 us (3%)
  local copies, waits for them, and re-layouts  4.58 us (3%)
    ppermute x10, starting transfers between devices, moved(): return lax.ppermute(value, ('x', 'y', 'half'), pairs)  54.9 us
    ppermute x10, waiting for transfers between devices, moved(): return lax.ppermute(value, ('x', 'y', 'half'), pairs)  54.7 us
    all_to_all x1, starting transfers between devices, local(): lax.all_to_all(row_copies, ('half', 'grp'), 0, 0, tiled=True)  12.9 us
    all_to_all x1, blocking collectives, local(): level_rows = lax.all_to_all(row_copies, ('x', 'y'), 0, 0, tiled=True)  11 us
    pallas_call x4, Pallas kernels, call(): pl.pallas_call(kernel, out_shape=outs, in_specs=[SMEM] * in_smem + [VMEM]...  10.5 us
    unnamed x14, local copies, waits for them, and re-layouts  3.99 us
  transfers between devices with their start and end apart: 11, of which 4 were waited for; matrix products, arithmetic and copies ran while one was open for 3% of the time, Pallas kernels for 5%

profile of v3, /device:TPU:62, one launch (start us, length us, event | category | flops | bytes accessed | tf_op | source)
XLA Modules:
  0.0 158.9 jit_solution(14505200017152573407)
XLA Ops:
  0.6 14.8 %collective-permute-start = (bf16[256,1152]{1,0:T(8,128)(2,1)}, bf16[256,1152]{1,0:T(8,128)(2,1)S(1)}, u32[]{:S(2)}, u32[]{:S(2)}) collective-permute-start(bf16[256,1152]{1,0:T(8,128)(2,1)} %texts.5), channel_id=1, source_target_pairs={{0,16},{16,0},{32,48},{48,32},{64,80},{80,64},{96,112},{112,96},{1... | collective-permute-start | bytes 1769480 | tf_op jit(solution)/shard_map/ppermute | solution.py:117
  15.5 3.1 %collective-permute-start.3 = (bf16[256,1152]{1,0:T(8,128)(2,1)}, bf16[256,1152]{1,0:T(8,128)(2,1)S(1)}, u32[]{:S(2)}, u32[]{:S(2)}) collective-permute-start(bf16[256,1152]{1,0:T(8,128)(2,1)} %mine.3), channel_id=1, source_target_pairs={{0,448},{16,464},{32,480},{48,496},{64,0},{80,16},{96,32},{112,48}... | collective-permute-start | bytes 1769480 | tf_op jit(solution)/shard_map/ppermute | solution.py:117
  18.6 6.2 %collective-permute-start.2 = (bf16[256,1152]{1,0:T(8,128)(2,1)}, bf16[256,1152]{1,0:T(8,128)(2,1)S(1)}, u32[]{:S(2)}, u32[]{:S(2)}) collective-permute-start(bf16[256,1152]{1,0:T(8,128)(2,1)} %mine.3), channel_id=1, source_target_pairs={{0,32},{16,48},{32,64},{48,80},{64,96},{80,112},{96,128},{112,144}... | collective-permute-start | bytes 1769480 | tf_op jit(solution)/shard_map/ppermute | solution.py:117
  24.8 1.9 %collective-permute-start.1 = (bf16[256,1152]{1,0:T(8,128)(2,1)}, bf16[256,1152]{1,0:T(8,128)(2,1)S(1)}, u32[]{:S(2)}, u32[]{:S(2)}) collective-permute-start(bf16[256,1152]{1,0:T(8,128)(2,1)} %mine.3), channel_id=1, source_target_pairs={{0,480},{16,496},{32,0},{48,16},{64,32},{80,48},{96,64},{112,80},{... | collective-permute-start | bytes 1769480 | tf_op jit(solution)/shard_map/ppermute | solution.py:117
  26.8 4.0 %collective-permute-start.4 = (bf16[256,1152]{1,0:T(8,128)(2,1)}, bf16[256,1152]{1,0:T(8,128)(2,1)S(1)}, u32[]{:S(2)}, u32[]{:S(2)}) collective-permute-start(bf16[256,1152]{1,0:T(8,128)(2,1)} %mine.3), channel_id=1, source_target_pairs={{0,64},{16,80},{32,96},{48,112},{64,128},{80,144},{96,160},{112,17... | collective-permute-start | bytes 1769480 | tf_op jit(solution)/shard_map/ppermute | solution.py:117
  32.1 0.1 pad_maximum_fusion.scalars
  32.2 0.0 copy-start
  32.2 1.1 copy-done
  33.3 0.0 copy-start.2
  33.3 1.1 copy-done.2
  34.3 0.0 copy-start.3
  34.4 1.5 first_pair.1
  35.8 31.3 %collective-permute-done.texts.far_texts = bf16[256,1152]{1,0:T(8,128)(2,1)S(1)} collective-permute-done((bf16[256,1152]{1,0:T(8,128)(2,1)}, bf16[256,1152]{1,0:T(8,128)(2,1)S(1)}, u32[]{:S(2)}, u32[]{:S(2)}) %collective-permute-start) | collective-permute-done | bytes 589856 | tf_op jit(solution)/shard_map/ppermute | solution.py:117
  67.2 0.0 collective-permute-done.3.ahead_2.refs_2_
  67.2 2.1 %collective-permute-done.2.behind.refs_1_ = bf16[256,1152]{1,0:T(8,128)(2,1)S(1)} collective-permute-done((bf16[256,1152]{1,0:T(8,128)(2,1)}, bf16[256,1152]{1,0:T(8,128)(2,1)S(1)}, u32[]{:S(2)}, u32[]{:S(2)}) %collective-permute-start.2) | collective-permute-done | bytes 589856 | tf_op jit(solution)/shard_map/ppermute | solution.py:117
  69.3 0.0 collective-permute-done.1.ahead.refs_0_
  69.3 0.0 collective-permute-done.4.behind_2.refs_3_
  69.3 0.0 copy-done.3
  69.3 0.0 copy-start.1
  69.3 2.9 %far_pairs.1 = (bf16[5,256,256]{2,1,0:T(8,128)(2,1)S(1)}, bf16[256,1152]{1,0:T(8,128)(2,1)S(1)}, f32[16,256]{1,0:T(8,128)S(1)}) custom-call(f32[3]{0:T(128)S(1)} %pad_maximum_fusion.scalars, bf16[256,1152]{1,0:T(8,128)(2,1)S(1)} %collective-permute-done.texts.far_texts, bf16[256,1152]{1,0:T(8,128)(2,1)S(1)} %copy-done.3, ...), custom_call_target="tpu_custom_call" | custom-call | bytes 589824 | tf_op jit(solution)/shard_map/far_pairs/pallas_call | solution.py:95
  72.2 10.0 %collective-permute-start.9 = (bf16[256,1152]{1,0:T(8,128)(2,1)S(1)}, bf16[256,1152]{1,0:T(8,128)(2,1)S(1)}, u32[]{:S(2)}, u32[]{:S(2)}) collective-permute-start(bf16[256,1152]{1,0:T(8,128)(2,1)S(1)} %get-tuple-element.45), channel_id=1, source_target_pairs={{0,16},{16,0},{32,48},{48,32},{64,80},{80,64},{96,112},{112,96},{1... | collective-permute-start | bytes 1769480 | tf_op jit(solution)/shard_map/ppermute | solution.py:117
  82.2 0.0 copy-done.1
  82.2 3.1 %own_pairs.1 = (bf16[4,256,256]{2,1,0:T(8,128)(2,1)S(1)}, f32[256,1152]{1,0:T(8,128)S(1)}, f32[16,128]{1,0:T(8,128)S(1)}) custom-call(f32[3]{0:T(128)S(1)} %pad_maximum_fusion.scalars, bf16[256,1152]{1,0:T(8,128)(2,1)S(1)} %copy-done.1, bf16[256,1152]{1,0:T(8,128)(2,1)S(1)} %collective-permute-done.1.ahead.refs_0_, ...), custom_call_target="tpu_custom_call" | custom-call | bytes 589824 | tf_op jit(solution)/shard_map/own_pairs/pallas_call | solution.py:95
  85.3 0.0 copy-start.4
  85.3 1.0 copy-done.4
  86.4 11.0 %all_to_all.20 = f32[16,1,128]{2,1,0:T(1,128)S(1)} all-to-all(f32[16,1,128]{2,1,0:T(1,128)S(1)} %bitcast.12), channel_id=1, replica_groups=mesh['x'=4,'y'=4,'half'=2,'grp'=16] {'x','y'}, dimensions={0} | all-to-all | bytes 16384 | tf_op jit(solution)/shard_map/all_to_all | solution.py:164
  97.3 0.0 copy-start.5
  97.3 3.0 %image_parts.1 = (f32[256,1152]{1,0:T(8,128)S(1)}, bf16[256,1152]{1,0:T(8,128)(2,1)}, bf16[256,1152]{1,0:T(8,128)(2,1)}, bf16[256,1152]{1,0:T(8,128)(2,1)}, bf16...) custom-call(bf16[256,1152]{1,0:T(8,128)(2,1)S(1)} %copy-done.1, bf16[256,256]{1,0:T(8,128)(2,1)S(1)} %get-tuple-element.26.first_slopes, ...), custom_call_target="tpu_custom_call" | custom-call | bytes 589824 | tf_op jit(solution)/shard_map/image_parts/pallas_call | solution.py:95
  100.3 5.5 %collective-permute-start.5 = (bf16[256,1152]{1,0:T(8,128)(2,1)}, bf16[256,1152]{1,0:T(8,128)(2,1)S(1)}, u32[]{:S(2)}, u32[]{:S(2)}) collective-permute-start(bf16[256,1152]{1,0:T(8,128)(2,1)} %get-tuple-element.39), channel_id=1, source_target_pairs={{480,0},{496,16},{0,32},{16,48},{32,64},{48,80},{64,96},{80,112},{... | collective-permute-start | bytes 1769480 | tf_op jit(solution)/shard_map/ppermute | solution.py:117
  105.8 1.9 %collective-permute-start.6 = (bf16[256,1152]{1,0:T(8,128)(2,1)}, bf16[256,1152]{1,0:T(8,128)(2,1)}, u32[]{:S(2)}, u32[]{:S(2)}) collective-permute-start(bf16[256,1152]{1,0:T(8,128)(2,1)} %get-tuple-element.40), channel_id=1, source_target_pairs={{32,0},{48,16},{64,32},{80,48},{96,64},{112,80},{128,96},{144,112}... | collective-permute-start | bytes 1769480 | tf_op jit(solution)/shard_map/ppermute | solution.py:117
  107.7 3.9 %collective-permute-start.7 = (bf16[256,1152]{1,0:T(8,128)(2,1)}, bf16[256,1152]{1,0:T(8,128)(2,1)}, u32[]{:S(2)}, u32[]{:S(2)}) collective-permute-start(bf16[256,1152]{1,0:T(8,128)(2,1)} %get-tuple-element.41), channel_id=1, source_target_pairs={{448,0},{464,16},{480,32},{496,48},{0,64},{16,80},{32,96},{48,112}... | collective-permute-start | bytes 1769480 | tf_op jit(solution)/shard_map/ppermute | solution.py:117
  111.7 3.4 %collective-permute-start.8 = (bf16[256,1152]{1,0:T(8,128)(2,1)S(1)}, bf16[256,1152]{1,0:T(8,128)(2,1)}, u32[]{:S(2)}, u32[]{:S(2)}) collective-permute-start(bf16[256,1152]{1,0:T(8,128)(2,1)S(1)} %get-tuple-element.42), channel_id=1, source_target_pairs={{64,0},{80,16},{96,32},{112,48},{128,64},{144,80},{160,96},{176,11... | collective-permute-start | bytes 1769480 | tf_op jit(solution)/shard_map/ppermute | solution.py:117
  115.1 13.2 %collective-permute-done.9 = bf16[256,1152]{1,0:T(8,128)(2,1)S(1)} collective-permute-done((bf16[256,1152]{1,0:T(8,128)(2,1)S(1)}, bf16[256,1152]{1,0:T(8,128)(2,1)S(1)}, u32[]{:S(2)}, u32[]{:S(2)}) %collective-permute-start.9) | collective-permute-done | bytes 589856 | tf_op jit(solution)/shard_map/ppermute | solution.py:117
  128.3 0.0 copy-start.6
  128.3 0.8 copy-done.6
  129.1 12.9 %all-to-all-start.1 = ((f32[32,1,128]{2,1,0:T(1,128)}), f32[32,1,128]{2,1,0:T(1,128)S(1)}, u32[]{:S(2)}, u32[]{:S(2)}) async-start(f32[32,1,128]{2,1,0:T(1,128)} %bitcast.6), calls=%async_computation.1 | async-start | bytes 32768 | tf_op jit(solution)/shard_map/all_to_all | solution.py:175
  142.1 0.0 copy-done.5
  142.1 2.0 %multiply_convert_fusion = bf16[256,1152]{1,0:T(8,128)(2,1)} fusion(f32[256,1152]{1,0:T(8,128)S(1)} %copy-done.5, bf16[256,1152]{1,0:T(8,128)(2,1)} %copy-done.6, f32[]{:T(128)} %bitcast), kind=kLoop, calls=%fused_computation | loop fusion | flops 1179648 | bytes 2359300 | tf_op jit(solution)/shard_map/convert_element_type | solution.py:184
  144.1 0.0 collective-permute-done.5
  144.1 0.0 collective-permute-done.6
  144.1 8.0 %collective-permute-done.7 = bf16[256,1152]{1,0:T(8,128)(2,1)} collective-permute-done((bf16[256,1152]{1,0:T(8,128)(2,1)}, bf16[256,1152]{1,0:T(8,128)(2,1)}, u32[]{:S(2)}, u32[]{:S(2)}) %collective-permute-start.7) | collective-permute-done | bytes 589856 | tf_op jit(solution)/shard_map/ppermute | solution.py:117
  152.1 0.0 collective-permute-done.8
  152.1 2.6 %multiply_convert_fusion.1 = bf16[256,1152]{1,0:T(8,128)(2,1)} fusion(bf16[256,1152]{1,0:T(8,128)(2,1)} %collective-permute-done.8, bf16[256,1152]{1,0:T(8,128)(2,1)} %collective-permute-done.7, bf16[256,1152]{1,0:T(8,128)(2,1)} %collective-permute-done.6, f32[256,1152]{1,0:T(8,128)S(1)} %get-tuple-element.38, ...), kind=kLoop, calls=%fused_computation.1 | loop fusion | flops 2949120 | bytes 4128772 | tf_op jit(solution)/shard_map/convert_element_type | solution.py:183
  154.7 0.0 all-to-all-done.1
  154.7 0.1 reduce_sum.9
  154.8 0.6 fusion
Async XLA Ops:
  0.6 66.5 %collective-permute-start = (bf16[256,1152]{1,0:T(8,128)(2,1)}, bf16[256,1152]{1,0:T(8,128)(2,1)S(1)}, u32[]{:S(2)}, u32[]{:S(2)}) collective-permute-start(bf16[256,1152]{1,0:T(8,128)(2,1)} %texts.5), channel_id=1, source_target_pairs={{0,16},{16,0},{32,48},{48,32},{64,80},{80,64},{96,112},{112,96},{1... | collective-permute-start | bytes 1769480 | tf_op jit(solution)/shard_map/ppermute | solution.py:117
  15.5 51.7 %collective-permute-start.3 = (bf16[256,1152]{1,0:T(8,128)(2,1)}, bf16[256,1152]{1,0:T(8,128)(2,1)S(1)}, u32[]{:S(2)}, u32[]{:S(2)}) collective-permute-start(bf16[256,1152]{1,0:T(8,128)(2,1)} %mine.3), channel_id=1, source_target_pairs={{0,448},{16,464},{32,480},{48,496},{64,0},{80,16},{96,32},{112,48}... | collective-permute-start | bytes 1769480 | tf_op jit(solution)/shard_map/ppermute | solution.py:117
  18.6 50.7 %collective-permute-start.2 = (bf16[256,1152]{1,0:T(8,128)(2,1)}, bf16[256,1152]{1,0:T(8,128)(2,1)S(1)}, u32[]{:S(2)}, u32[]{:S(2)}) collective-permute-start(bf16[256,1152]{1,0:T(8,128)(2,1)} %mine.3), channel_id=1, source_target_pairs={{0,32},{16,48},{32,64},{48,80},{64,96},{80,112},{96,128},{112,144}... | collective-permute-start | bytes 1769480 | tf_op jit(solution)/shard_map/ppermute | solution.py:117
  24.8 44.5 %collective-permute-start.1 = (bf16[256,1152]{1,0:T(8,128)(2,1)}, bf16[256,1152]{1,0:T(8,128)(2,1)S(1)}, u32[]{:S(2)}, u32[]{:S(2)}) collective-permute-start(bf16[256,1152]{1,0:T(8,128)(2,1)} %mine.3), channel_id=1, source_target_pairs={{0,480},{16,496},{32,0},{48,16},{64,32},{80,48},{96,64},{112,80},{... | collective-permute-start | bytes 1769480 | tf_op jit(solution)/shard_map/ppermute | solution.py:117
  26.8 42.5 %collective-permute-start.4 = (bf16[256,1152]{1,0:T(8,128)(2,1)}, bf16[256,1152]{1,0:T(8,128)(2,1)S(1)}, u32[]{:S(2)}, u32[]{:S(2)}) collective-permute-start(bf16[256,1152]{1,0:T(8,128)(2,1)} %mine.3), channel_id=1, source_target_pairs={{0,64},{16,80},{32,96},{48,112},{64,128},{80,144},{96,160},{112,17... | collective-permute-start | bytes 1769480 | tf_op jit(solution)/shard_map/ppermute | solution.py:117
  32.2 1.1 copy-start
  33.3 1.1 copy-start.2
  34.3 34.9 %copy-start.3 = (bf16[256,1152]{1,0:T(8,128)(2,1)S(1)}, bf16[256,1152]{1,0:T(8,128)(2,1)}, u32[]{:S(2)}) copy-start(bf16[256,1152]{1,0:T(8,128)(2,1)} %mine.3) | copy-start | bytes 1769476
  69.3 12.9 %copy-start.1 = (bf16[256,1152]{1,0:T(8,128)(2,1)S(1)}, bf16[256,1152]{1,0:T(8,128)(2,1)}, u32[]{:S(2)}) copy-start(bf16[256,1152]{1,0:T(8,128)(2,1)} %texts.5) | copy-start | bytes 1769476
  72.2 56.1 %collective-permute-start.9 = (bf16[256,1152]{1,0:T(8,128)(2,1)S(1)}, bf16[256,1152]{1,0:T(8,128)(2,1)S(1)}, u32[]{:S(2)}, u32[]{:S(2)}) collective-permute-start(bf16[256,1152]{1,0:T(8,128)(2,1)S(1)} %get-tuple-element.45), channel_id=1, source_target_pairs={{0,16},{16,0},{32,48},{48,32},{64,80},{80,64},{96,112},{112,96},{1... | collective-permute-start | bytes 1769480 | tf_op jit(solution)/shard_map/ppermute | solution.py:117
  85.3 1.0 copy-start.4
  97.3 44.8 %copy-start.5 = (f32[256,1152]{1,0:T(8,128)S(1)}, f32[256,1152]{1,0:T(8,128)}, u32[]{:S(2)}) copy-start(f32[256,1152]{1,0:T(8,128)} %copy-done.4) | copy-start | bytes 3538948
  100.3 43.8 %collective-permute-start.5 = (bf16[256,1152]{1,0:T(8,128)(2,1)}, bf16[256,1152]{1,0:T(8,128)(2,1)S(1)}, u32[]{:S(2)}, u32[]{:S(2)}) collective-permute-start(bf16[256,1152]{1,0:T(8,128)(2,1)} %get-tuple-element.39), channel_id=1, source_target_pairs={{480,0},{496,16},{0,32},{16,48},{32,64},{48,80},{64,96},{80,112},{... | collective-permute-start | bytes 1769480 | tf_op jit(solution)/shard_map/ppermute | solution.py:117
  105.8 38.3 %collective-permute-start.6 = (bf16[256,1152]{1,0:T(8,128)(2,1)}, bf16[256,1152]{1,0:T(8,128)(2,1)}, u32[]{:S(2)}, u32[]{:S(2)}) collective-permute-start(bf16[256,1152]{1,0:T(8,128)(2,1)} %get-tuple-element.40), channel_id=1, source_target_pairs={{32,0},{48,16},{64,32},{80,48},{96,64},{112,80},{128,96},{144,112}... | collective-permute-start | bytes 1769480 | tf_op jit(solution)/shard_map/ppermute | solution.py:117
  107.7 44.4 %collective-permute-start.7 = (bf16[256,1152]{1,0:T(8,128)(2,1)}, bf16[256,1152]{1,0:T(8,128)(2,1)}, u32[]{:S(2)}, u32[]{:S(2)}) collective-permute-start(bf16[256,1152]{1,0:T(8,128)(2,1)} %get-tuple-element.41), channel_id=1, source_target_pairs={{448,0},{464,16},{480,32},{496,48},{0,64},{16,80},{32,96},{48,112}... | collective-permute-start | bytes 1769480 | tf_op jit(solution)/shard_map/ppermute | solution.py:117
  111.7 40.5 %collective-permute-start.8 = (bf16[256,1152]{1,0:T(8,128)(2,1)S(1)}, bf16[256,1152]{1,0:T(8,128)(2,1)}, u32[]{:S(2)}, u32[]{:S(2)}) collective-permute-start(bf16[256,1152]{1,0:T(8,128)(2,1)S(1)} %get-tuple-element.42), channel_id=1, source_target_pairs={{64,0},{80,16},{96,32},{112,48},{128,64},{144,80},{160,96},{176,11... | collective-permute-start | bytes 1769480 | tf_op jit(solution)/shard_map/ppermute | solution.py:117
  128.3 0.8 copy-start.6
  129.1 25.6 %all-to-all-start.1 = ((f32[32,1,128]{2,1,0:T(1,128)}), f32[32,1,128]{2,1,0:T(1,128)S(1)}, u32[]{:S(2)}, u32[]{:S(2)}) async-start(f32[32,1,128]{2,1,0:T(1,128)} %bitcast.6), calls=%async_computation.1 | async-start | bytes 32768 | tf_op jit(solution)/shard_map/all_to_all | solution.py:175

commit v4 on v3

v4 whole, which is shorter than its diff:
```python
import jax
import jax.numpy as jnp
from jax import lax
from jax.experimental import pallas as pl
from jax.experimental.pallas import tpu as pltpu
from jax.sharding import Mesh
from jax.sharding import PartitionSpec as P

F32, BF16 = jnp.float32, jnp.bfloat16
VMEM = pl.BlockSpec(memory_space=pltpu.VMEM)
SMEM = pl.BlockSpec(memory_space=pltpu.SMEM)
PARAMS = pltpu.CompilerParams(vmem_limit_bytes=48 * 1024 * 1024)


def dot(left, right, left_dim, right_dim):
    return lax.dot_general(
        left, right, (((left_dim,), (right_dim,)), ((), ())), preferred_element_type=F32
    )


def fold(tile):
    return jnp.sum(tile.reshape(-1, 8, tile.shape[-1]), axis=0)


def score(scalars, texts, images, on_diagonal):
    products = dot(texts, images, 1, 1)
    slopes = jax.nn.sigmoid(scalars[0] * products + scalars[1])
    if on_diagonal:
        rows = lax.broadcasted_iota(jnp.int32, slopes.shape, 0)
        columns = lax.broadcasted_iota(jnp.int32, slopes.shape, 1)
        slopes = slopes - jnp.where(rows == columns, 1.0, 0.0)
    return slopes.astype(BF16), fold(slopes), fold(slopes * products)


def first_kernel(scalars, texts, mine, slopes_out, grad_out, sums_out):
    half, bias_sum, scale_sum = score(scalars, texts[...], mine[...], True)
    slopes_out[...] = half
    grad_out[...] = dot(half, mine[...], 1, 0)
    sums_out[0:8] = bias_sum
    sums_out[8:16] = scale_sum


def own_kernel(first_grad, own_slopes, ahead, behind, outer, inner, grad_out):
    grad = first_grad[...]
    for slot, images in enumerate((ahead, behind, outer, inner)):
        grad = grad + dot(own_slopes[slot], images[...], 1, 0)
    grad_out[...] = grad


def lane_row(bias_sum, scale_sum):
    lane = lax.broadcasted_iota(jnp.int32, (1, 128), 1)
    return jnp.where(lane == 0, bias_sum, jnp.where(lane == 1, scale_sum, 0.0))


def far_kernel(scalars, texts, mine, ahead, behind, outer, sums, slopes_out, grad_out, sums_out):
    bias_sum, scale_sum, grad = sums[0:8], sums[8:16], None
    for slot, images in enumerate((mine, ahead, behind, outer)):
        half, bias_part, scale_part = score(scalars, texts[...], images[...], False)
        part = dot(half, images[...], 1, 0)
        grad = part if grad is None else grad + part
        bias_sum, scale_sum = bias_sum + bias_part, scale_sum + scale_part
        slopes_out[slot] = half
    grad_out[...] = grad.astype(BF16)
    sums_out[0:8] = bias_sum
    sums_out[8:16] = scale_sum


def images_kernel(
    scalars, texts, ahead, behind, outer, inner, sums, first_slopes, far_texts, far_slopes, own_out, row_out, *outs
):
    bias_sum, scale_sum = sums[0:8], sums[8:16]
    near = (None, ahead, behind, outer, inner)
    for slot in (3, 4, 1, 2, 0):
        if slot == 0:
            half = first_slopes[...]
        else:
            half, bias_part, scale_part = score(scalars, texts[...], near[slot][...], False)
            bias_sum, scale_sum = bias_sum + bias_part, scale_sum + scale_part
            own_out[slot - 1] = half
        grad = dot(half, texts[...], 0, 0)
        if slot < 4:
            grad = grad + dot(far_slopes[slot], far_texts[...], 0, 0)
        outs[slot][...] = grad.astype(outs[slot].dtype)
    row_out[...] = jnp.broadcast_to(lane_row(jnp.sum(bias_sum), jnp.sum(scale_sum)), row_out.shape)


def column_kernel(rows, *refs):
    refs[-1][...] = jnp.broadcast_to(jnp.sum(rows[...], axis=0, keepdims=True), refs[-1].shape)


def shape(rows, columns, kind):
    return jax.ShapeDtypeStruct((rows, columns), kind)


def cost(moved):
    return pl.CostEstimate(flops=0, bytes_accessed=moved, transcendentals=0)


def call(kernel, name, outs, in_smem, args, moved):
    return pl.pallas_call(
        kernel,
        out_shape=outs,
        in_specs=[SMEM] * in_smem + [VMEM] * (len(args) - in_smem),
        out_specs=(VMEM,) * len(outs),
        compiler_params=PARAMS,
        cost_estimate=pl.CostEstimate(flops=0, bytes_accessed=moved, transcendentals=0),
        name=name,
    )(*args)


def local(images, texts, log_temp, bias):
    rows, width = images.shape
    columns_count, halves = lax.axis_size(("x", "y")), lax.axis_size("half")
    in_column = halves * lax.axis_size("grp")
    stops = columns_count * halves
    scale = jnp.exp(log_temp[0])
    scalars = jnp.stack([scale, bias[0]])
    block = rows * width * 2

    def moved(value, pairs):
        return lax.ppermute(value, ("x", "y", "half"), pairs)

    def columns(count):
        return [(s, (s - 2 * count) % stops) for s in range(stops)]

    def back(pairs):
        return [(b, a) for a, b in pairs]

    flip = [(s, s ^ 1) for s in range(stops)]
    outward = [(s, (s - 4 * (1 - 2 * (s % 2))) % stops) for s in range(stops)]
    ways = (columns(1), columns(-1), outward, back(outward))

    far_texts = moved(texts, flip)
    ahead, behind, outer, inner = [moved(images, way) for way in ways]
    first_slopes, text_first, sums = call(
        first_kernel,
        "first_pair",
        (shape(rows, rows, BF16), shape(rows, width, F32), shape(16, rows, F32)),
        1,
        (scalars, texts, images),
        100 * block,
    )
    far_texts, ahead, behind, outer = lax.optimization_barrier((far_texts, ahead, behind, outer))
    near = (ahead, behind, outer, inner)
    far_slopes, far_grad, sums = call(
        far_kernel,
        "far_pairs",
        (jax.ShapeDtypeStruct((4, rows, rows), BF16), shape(rows, width, BF16), shape(16, rows, F32)),
        1,
        (scalars, far_texts, images, *near[:3], sums),
        block,
    )
    text_back = moved(far_grad, flip)
    own_slopes, row_copies, image_own, *image_parts = call(
        images_kernel,
        "image_parts",
        (jax.ShapeDtypeStruct((4, rows, rows), BF16), shape(in_column, 128, F32), shape(rows, width, F32))
        + (shape(rows, width, BF16),) * 4,
        1,
        (scalars, texts, *near, sums, first_slopes, far_texts, far_slopes),
        block,
    )
    image_back = [moved(part, back(way)) for part, way in zip(image_parts, ways, strict=True)]
    own_slopes, text_first, image_own = lax.optimization_barrier((own_slopes, text_first, image_own))
    (text_own,) = call(
        own_kernel, "own_texts", (shape(rows, width, F32),), 0, (text_first, own_slopes, *near), block
    )
    row_copies, text_own = lax.optimization_barrier((row_copies, text_own))
    column_rows = lax.all_to_all(row_copies, ("half", "grp"), 0, 0, tiled=True)
    row_copies = pl.pallas_call(
        column_kernel,
        out_shape=shape(columns_count, 128, F32),
        in_specs=[VMEM] * 3,
        out_specs=VMEM,
        compiler_params=PARAMS,
        name="column_sums",
    )(column_rows, text_back, image_back[0])
    sums_all = jnp.sum(lax.all_to_all(row_copies, ("x", "y"), 0, 0, tiled=True), axis=0)

    batch_rows = rows * columns_count * in_column
    bias_grad = (sums_all[0] / batch_rows).reshape(1)
    temp_grad = (scale * sums_all[1] / batch_rows).reshape(1)
    image_sum = image_own
    for part in image_back:
        image_sum = image_sum + part.astype(F32)
    text_grad = (scale * (text_own + text_back.astype(F32))).astype(BF16)
    image_grad = (scale * image_sum).astype(BF16)
    return image_grad, text_grad, bias_grad, temp_grad


def solution(mesh):
    x_y_half = (4, 4, 2)
    fine = Mesh(mesh.devices.reshape(*x_y_half, -1), ("x", "y", "half", "grp"))
    split = P(("x", "y", "half", "grp"), None)
    return jax.shard_map(
        local, mesh=fine, in_specs=(split, split, P(), P()), out_specs=(split, split, P(), P()), check_vma=False
    )
```

time: 160 us -> 156 us (0.975)
  the two profiles are of different devices: /device:TPU:62 before, /device:TPU:1 now
where the time goes in v4:
time: 156 us; the launch traced here: 155 us
  starting transfers between devices  80.8 us (52%)
  blocking collectives  34.3 us (22%)
  waiting for transfers between devices  14.3 us (9%)
  Pallas kernels  11.2 us (7%)
  between operations  5.62 us (4%)
  local copies, waits for them, and re-layouts  4.6 us (3%)
  other arithmetic  4.06 us (3%)
    ppermute x10, starting transfers between devices, moved(): return lax.ppermute(value, ('x', 'y', 'half'), pairs)  74.6 us
    all_to_all x1, blocking collectives, local(): column_rows = lax.all_to_all(row_copies, ('half', 'grp'), 0, 0, tiled=True)  34.3 us
    ppermute x10, waiting for transfers between devices, moved(): return lax.ppermute(value, ('x', 'y', 'half'), pairs)  11.8 us
    pallas_call x4, Pallas kernels, call(): pl.pallas_call(kernel, out_shape=outs, in_specs=[SMEM] * in_smem + [VMEM]...  10.6 us
    all_to_all x1, starting transfers between devices, local(): lax.all_to_all(row_copies, ('x', 'y'), 0, 0, tiled=True)  6.19 us
    unnamed x14, local copies, waits for them, and re-layouts  4.01 us
  transfers between devices with their start and end apart: 11, of which 2 were waited for; matrix products, arithmetic and copies ran while one was open for 3% of the time, Pallas kernels for 7%

profile of v4, /device:TPU:1, one launch (start us, length us, event | category | flops | bytes accessed | tf_op | source)
XLA Modules:
  0.0 154.8 jit_solution(13012969011155849271)
XLA Ops:
  0.6 16.3 %collective-permute-start = (bf16[256,1152]{1,0:T(8,128)(2,1)}, bf16[256,1152]{1,0:T(8,128)(2,1)S(1)}, u32[]{:S(2)}, u32[]{:S(2)}) collective-permute-start(bf16[256,1152]{1,0:T(8,128)(2,1)} %texts.3), channel_id=1, source_target_pairs={{0,16},{16,0},{32,48},{48,32},{64,80},{80,64},{96,112},{112,96},{1... | collective-permute-start | bytes 1769480 | tf_op jit(solution)/shard_map/ppermute | solution.py:121
  16.9 7.0 %collective-permute-start.3 = (bf16[256,1152]{1,0:T(8,128)(2,1)}, bf16[256,1152]{1,0:T(8,128)(2,1)S(1)}, u32[]{:S(2)}, u32[]{:S(2)}) collective-permute-start(bf16[256,1152]{1,0:T(8,128)(2,1)} %mine.3), channel_id=1, source_target_pairs={{0,448},{16,80},{32,480},{48,112},{64,0},{80,144},{96,32},{112,176... | collective-permute-start | bytes 1769480 | tf_op jit(solution)/shard_map/ppermute | solution.py:121
  23.9 2.3 %collective-permute-start.2 = (bf16[256,1152]{1,0:T(8,128)(2,1)}, bf16[256,1152]{1,0:T(8,128)(2,1)S(1)}, u32[]{:S(2)}, u32[]{:S(2)}) collective-permute-start(bf16[256,1152]{1,0:T(8,128)(2,1)} %mine.3), channel_id=1, source_target_pairs={{0,32},{16,48},{32,64},{48,80},{64,96},{80,112},{96,128},{112,144}... | collective-permute-start | bytes 1769480 | tf_op jit(solution)/shard_map/ppermute | solution.py:121
  26.3 6.3 %collective-permute-start.1 = (bf16[256,1152]{1,0:T(8,128)(2,1)}, bf16[256,1152]{1,0:T(8,128)(2,1)S(1)}, u32[]{:S(2)}, u32[]{:S(2)}) collective-permute-start(bf16[256,1152]{1,0:T(8,128)(2,1)} %mine.3), channel_id=1, source_target_pairs={{0,480},{16,496},{32,0},{48,16},{64,32},{80,48},{96,64},{112,80},{... | collective-permute-start | bytes 1769480 | tf_op jit(solution)/shard_map/ppermute | solution.py:121
  32.6 1.9 %collective-permute-start.4 = (bf16[256,1152]{1,0:T(8,128)(2,1)}, bf16[256,1152]{1,0:T(8,128)(2,1)S(1)}, u32[]{:S(2)}, u32[]{:S(2)}) collective-permute-start(bf16[256,1152]{1,0:T(8,128)(2,1)} %mine.3), channel_id=1, source_target_pairs={{448,0},{80,16},{480,32},{112,48},{0,64},{144,80},{32,96},{176,112... | collective-permute-start | bytes 1769480 | tf_op jit(solution)/shard_map/ppermute | solution.py:121
  35.8 0.1 pad_maximum_fusion.scalars
  35.9 0.0 copy-start.3
  35.9 1.1 copy-done.3
  37.0 0.0 copy-start.5
  37.0 1.1 copy-done.5
  38.0 0.0 copy-start.6
  38.0 1.5 first_pair.1
  39.5 0.0 collective-permute-done.texts.far_texts
  39.5 0.0 copy-start.2
  39.5 0.0 collective-permute-done.3.outer
  39.5 11.8 %collective-permute-done.2.behind = bf16[256,1152]{1,0:T(8,128)(2,1)S(1)} collective-permute-done((bf16[256,1152]{1,0:T(8,128)(2,1)}, bf16[256,1152]{1,0:T(8,128)(2,1)S(1)}, u32[]{:S(2)}, u32[]{:S(2)}) %collective-permute-start.2) | collective-permute-done | bytes 589856 | tf_op jit(solution)/shard_map/ppermute | solution.py:121
  51.4 0.0 collective-permute-done.1.ahead
  51.4 0.0 copy-done.6
  51.4 0.0 copy-start.4
  51.4 2.9 %far_pairs.1 = (bf16[4,256,256]{2,1,0:T(8,128)(2,1)S(1)}, bf16[256,1152]{1,0:T(8,128)(2,1)S(1)}, f32[16,256]{1,0:T(8,128)S(1)}) custom-call(f32[2]{0:T(128)S(1)} %pad_maximum_fusion.scalars, bf16[256,1152]{1,0:T(8,128)(2,1)S(1)} %collective-permute-done.texts.far_texts, bf16[256,1152]{1,0:T(8,128)(2,1)S(1)} %copy-done.6, ...), custom_call_target="tpu_custom_call" | custom-call | bytes 589824 | tf_op jit(solution)/shard_map/far_pairs/pallas_call | solution.py:100
  54.3 0.0 copy-done.2
  54.3 23.3 %collective-permute-start.9 = (bf16[256,1152]{1,0:T(8,128)(2,1)S(1)}, bf16[256,1152]{1,0:T(8,128)(2,1)S(1)}, u32[]{:S(2)}, u32[]{:S(2)}) collective-permute-start(bf16[256,1152]{1,0:T(8,128)(2,1)S(1)} %get-tuple-element.46), channel_id=1, source_target_pairs={{0,16},{16,0},{32,48},{48,32},{64,80},{80,64},{96,112},{112,96},{1... | collective-permute-start | bytes 1769480 | tf_op jit(solution)/shard_map/ppermute | solution.py:121
  77.6 0.0 collective-permute-done.4.inner
  77.6 0.0 copy-start
  77.6 0.8 copy-done
  78.4 0.0 copy-done.4
  78.4 5.3 %image_parts.1 = (bf16[4,256,256]{2,1,0:T(8,128)(2,1)S(1)}, f32[32,128]{1,0:T(8,128)S(1)}, f32[256,1152]{1,0:T(8,128)}, bf16[256,1152]{1,0:T(8,128)(2,1)S(1)}, b...) custom-call(f32[2]{0:T(128)S(1)} %pad_maximum_fusion.scalars, ...), custom_call_target="tpu_custom_call" | custom-call | bytes 589824 | tf_op jit(solution)/shard_map/image_parts/pallas_call | solution.py:100
  83.8 1.9 %collective-permute-start.5 = (bf16[256,1152]{1,0:T(8,128)(2,1)S(1)}, bf16[256,1152]{1,0:T(8,128)(2,1)S(1)}, u32[]{:S(2)}, u32[]{:S(2)}) collective-permute-start(bf16[256,1152]{1,0:T(8,128)(2,1)S(1)} %get-tuple-element.38), channel_id=1, source_target_pairs={{480,0},{496,16},{0,32},{16,48},{32,64},{48,80},{64,96},{80,112},{... | collective-permute-start | bytes 1769480 | tf_op jit(solution)/shard_map/ppermute | solution.py:121
  85.7 6.7 %collective-permute-start.6 = (bf16[256,1152]{1,0:T(8,128)(2,1)}, bf16[256,1152]{1,0:T(8,128)(2,1)}, u32[]{:S(2)}, u32[]{:S(2)}) collective-permute-start(bf16[256,1152]{1,0:T(8,128)(2,1)} %get-tuple-element.39), channel_id=1, source_target_pairs={{32,0},{48,16},{64,32},{80,48},{96,64},{112,80},{128,96},{144,112}... | collective-permute-start | bytes 1769480 | tf_op jit(solution)/shard_map/ppermute | solution.py:121
  92.4 1.9 %collective-permute-start.7 = (bf16[256,1152]{1,0:T(8,128)(2,1)S(1)}, bf16[256,1152]{1,0:T(8,128)(2,1)}, u32[]{:S(2)}, u32[]{:S(2)}) collective-permute-start(bf16[256,1152]{1,0:T(8,128)(2,1)S(1)} %get-tuple-element.40), channel_id=1, source_target_pairs={{448,0},{80,16},{480,32},{112,48},{0,64},{144,80},{32,96},{176,112... | collective-permute-start | bytes 1769480 | tf_op jit(solution)/shard_map/ppermute | solution.py:121
  94.3 7.0 %collective-permute-start.8 = (bf16[256,1152]{1,0:T(8,128)(2,1)S(1)}, bf16[256,1152]{1,0:T(8,128)(2,1)}, u32[]{:S(2)}, u32[]{:S(2)}) collective-permute-start(bf16[256,1152]{1,0:T(8,128)(2,1)S(1)} %get-tuple-element.41), channel_id=1, source_target_pairs={{0,448},{16,80},{32,480},{48,112},{64,0},{80,144},{96,32},{112,176... | collective-permute-start | bytes 1769480 | tf_op jit(solution)/shard_map/ppermute | solution.py:121
  101.3 0.0 copy-start.1
  101.3 1.1 copy-done.1
  102.4 0.8 own_texts.1
  103.2 34.3 %all_to_all.20 = f32[32,1,128]{2,1,0:T(1,128)S(1)} all-to-all(f32[32,1,128]{2,1,0:T(1,128)S(1)} %bitcast.11), channel_id=1, replica_groups=mesh['x'=4,'y'=4,'half'=2,'grp'=16] {'half','grp'}, dimensions={0} | all-to-all | bytes 32768 | tf_op jit(solution)/shard_map/all_to_all | solution.py:169
  137.5 0.0 collective-permute-done.9.refs_0_
  137.5 0.0 collective-permute-done.5.refs_1_
  137.5 0.6 column_sums.1
  138.1 6.2 %all-to-all-start.1 = ((f32[16,1,128]{2,1,0:T(1,128)}), f32[16,1,128]{2,1,0:T(1,128)S(1)}, u32[]{:S(2)}, u32[]{:S(2)}) async-start(f32[16,1,128]{2,1,0:T(1,128)} %bitcast.5), calls=%async_computation.1 | async-start | bytes 16384 | tf_op jit(solution)/shard_map/all_to_all | solution.py:178
  144.3 0.0 collective-permute-done.6
  144.3 0.0 collective-permute-done.7
  144.4 0.0 collective-permute-done.8
  144.4 3.0 %multiply_convert_fusion.1 = bf16[256,1152]{1,0:T(8,128)(2,1)} fusion(bf16[256,1152]{1,0:T(8,128)(2,1)} %collective-permute-done.8, bf16[256,1152]{1,0:T(8,128)(2,1)} %collective-permute-done.7, bf16[256,1152]{1,0:T(8,128)(2,1)} %collective-permute-done.6, f32[256,1152]{1,0:T(8,128)} %get-tuple-element.37, ...), kind=kLoop, calls=%fused_computation.1 | loop fusion | flops 2949120 | bytes 4128772 | tf_op jit(solution)/shard_map/convert_element_type | solution.py:187
  147.4 1.0 multiply_convert_fusion
  148.3 2.4 %all-to-all-done.1 = f32[16,1,128]{2,1,0:T(1,128)S(1)} async-done(((f32[16,1,128]{2,1,0:T(1,128)}), f32[16,1,128]{2,1,0:T(1,128)S(1)}, u32[]{:S(2)}, u32[]{:S(2)}) %all-to-all-start.1) | async-done | bytes 8224 | tf_op jit(solution)/shard_map/all_to_all | solution.py:178
  150.8 0.6 fusion
  (1 shorter events, 0.0 us)
Async XLA Ops:
  0.6 38.9 %collective-permute-start = (bf16[256,1152]{1,0:T(8,128)(2,1)}, bf16[256,1152]{1,0:T(8,128)(2,1)S(1)}, u32[]{:S(2)}, u32[]{:S(2)}) collective-permute-start(bf16[256,1152]{1,0:T(8,128)(2,1)} %texts.3), channel_id=1, source_target_pairs={{0,16},{16,0},{32,48},{48,32},{64,80},{80,64},{96,112},{112,96},{1... | collective-permute-start | bytes 1769480 | tf_op jit(solution)/shard_map/ppermute | solution.py:121
  16.9 22.6 %collective-permute-start.3 = (bf16[256,1152]{1,0:T(8,128)(2,1)}, bf16[256,1152]{1,0:T(8,128)(2,1)S(1)}, u32[]{:S(2)}, u32[]{:S(2)}) collective-permute-start(bf16[256,1152]{1,0:T(8,128)(2,1)} %mine.3), channel_id=1, source_target_pairs={{0,448},{16,80},{32,480},{48,112},{64,0},{80,144},{96,32},{112,176... | collective-permute-start | bytes 1769480 | tf_op jit(solution)/shard_map/ppermute | solution.py:121
  23.9 27.4 %collective-permute-start.2 = (bf16[256,1152]{1,0:T(8,128)(2,1)}, bf16[256,1152]{1,0:T(8,128)(2,1)S(1)}, u32[]{:S(2)}, u32[]{:S(2)}) collective-permute-start(bf16[256,1152]{1,0:T(8,128)(2,1)} %mine.3), channel_id=1, source_target_pairs={{0,32},{16,48},{32,64},{48,80},{64,96},{80,112},{96,128},{112,144}... | collective-permute-start | bytes 1769480 | tf_op jit(solution)/shard_map/ppermute | solution.py:121
  26.3 25.1 %collective-permute-start.1 = (bf16[256,1152]{1,0:T(8,128)(2,1)}, bf16[256,1152]{1,0:T(8,128)(2,1)S(1)}, u32[]{:S(2)}, u32[]{:S(2)}) collective-permute-start(bf16[256,1152]{1,0:T(8,128)(2,1)} %mine.3), channel_id=1, source_target_pairs={{0,480},{16,496},{32,0},{48,16},{64,32},{80,48},{96,64},{112,80},{... | collective-permute-start | bytes 1769480 | tf_op jit(solution)/shard_map/ppermute | solution.py:121
  32.6 45.1 %collective-permute-start.4 = (bf16[256,1152]{1,0:T(8,128)(2,1)}, bf16[256,1152]{1,0:T(8,128)(2,1)S(1)}, u32[]{:S(2)}, u32[]{:S(2)}) collective-permute-start(bf16[256,1152]{1,0:T(8,128)(2,1)} %mine.3), channel_id=1, source_target_pairs={{448,0},{80,16},{480,32},{112,48},{0,64},{144,80},{32,96},{176,112... | collective-permute-start | bytes 1769480 | tf_op jit(solution)/shard_map/ppermute | solution.py:121
  35.9 1.1 copy-start.3
  37.0 1.1 copy-start.5
  38.0 13.3 %copy-start.6 = (bf16[256,1152]{1,0:T(8,128)(2,1)S(1)}, bf16[256,1152]{1,0:T(8,128)(2,1)}, u32[]{:S(2)}) copy-start(bf16[256,1152]{1,0:T(8,128)(2,1)} %mine.3) | copy-start | bytes 1769476
  39.5 14.8 %copy-start.2 = (bf16[256,1152]{1,0:T(8,128)(2,1)}, bf16[256,1152]{1,0:T(8,128)(2,1)S(1)}, u32[]{:S(2)}) copy-start(bf16[256,1152]{1,0:T(8,128)(2,1)S(1)} %collective-permute-done.texts.far_texts) | copy-start | bytes 1769476
  51.4 27.1 %copy-start.4 = (bf16[256,1152]{1,0:T(8,128)(2,1)S(1)}, bf16[256,1152]{1,0:T(8,128)(2,1)}, u32[]{:S(2)}) copy-start(bf16[256,1152]{1,0:T(8,128)(2,1)} %texts.3) | copy-start | bytes 1769476
  54.3 83.2 %collective-permute-start.9 = (bf16[256,1152]{1,0:T(8,128)(2,1)S(1)}, bf16[256,1152]{1,0:T(8,128)(2,1)S(1)}, u32[]{:S(2)}, u32[]{:S(2)}) collective-permute-start(bf16[256,1152]{1,0:T(8,128)(2,1)S(1)} %get-tuple-element.46), channel_id=1, source_target_pairs={{0,16},{16,0},{32,48},{48,32},{64,80},{80,64},{96,112},{112,96},{1... | collective-permute-start | bytes 1769480 | tf_op jit(solution)/shard_map/ppermute | solution.py:121
  77.6 0.8 copy-start
  83.8 53.7 %collective-permute-start.5 = (bf16[256,1152]{1,0:T(8,128)(2,1)S(1)}, bf16[256,1152]{1,0:T(8,128)(2,1)S(1)}, u32[]{:S(2)}, u32[]{:S(2)}) collective-permute-start(bf16[256,1152]{1,0:T(8,128)(2,1)S(1)} %get-tuple-element.38), channel_id=1, source_target_pairs={{480,0},{496,16},{0,32},{16,48},{32,64},{48,80},{64,96},{80,112},{... | collective-permute-start | bytes 1769480 | tf_op jit(solution)/shard_map/ppermute | solution.py:121
  85.7 58.6 %collective-permute-start.6 = (bf16[256,1152]{1,0:T(8,128)(2,1)}, bf16[256,1152]{1,0:T(8,128)(2,1)}, u32[]{:S(2)}, u32[]{:S(2)}) collective-permute-start(bf16[256,1152]{1,0:T(8,128)(2,1)} %get-tuple-element.39), channel_id=1, source_target_pairs={{32,0},{48,16},{64,32},{80,48},{96,64},{112,80},{128,96},{144,112}... | collective-permute-start | bytes 1769480 | tf_op jit(solution)/shard_map/ppermute | solution.py:121
  92.4 51.9 %collective-permute-start.7 = (bf16[256,1152]{1,0:T(8,128)(2,1)S(1)}, bf16[256,1152]{1,0:T(8,128)(2,1)}, u32[]{:S(2)}, u32[]{:S(2)}) collective-permute-start(bf16[256,1152]{1,0:T(8,128)(2,1)S(1)} %get-tuple-element.40), channel_id=1, source_target_pairs={{448,0},{80,16},{480,32},{112,48},{0,64},{144,80},{32,96},{176,112... | collective-permute-start | bytes 1769480 | tf_op jit(solution)/shard_map/ppermute | solution.py:121
  94.3 50.0 %collective-permute-start.8 = (bf16[256,1152]{1,0:T(8,128)(2,1)S(1)}, bf16[256,1152]{1,0:T(8,128)(2,1)}, u32[]{:S(2)}, u32[]{:S(2)}) collective-permute-start(bf16[256,1152]{1,0:T(8,128)(2,1)S(1)} %get-tuple-element.41), channel_id=1, source_target_pairs={{0,448},{16,80},{32,480},{48,112},{64,0},{80,144},{96,32},{112,176... | collective-permute-start | bytes 1769480 | tf_op jit(solution)/shard_map/ppermute | solution.py:121
  101.3 1.1 copy-start.1
  138.1 12.6 %all-to-all-start.1 = ((f32[16,1,128]{2,1,0:T(1,128)}), f32[16,1,128]{2,1,0:T(1,128)S(1)}, u32[]{:S(2)}, u32[]{:S(2)}) async-start(f32[16,1,128]{2,1,0:T(1,128)} %bitcast.5), calls=%async_computation.1 | async-start | bytes 16384 | tf_op jit(solution)/shard_map/all_to_all | solution.py:178

commit v5 on v4

--- a/solution.py
+++ b/solution.py
@@ -140,7 +140,7 @@
         (scalars, texts, images),
         100 * block,
     )
-    far_texts, ahead, behind, outer = lax.optimization_barrier((far_texts, ahead, behind, outer))
+    far_texts, outer, ahead, behind = lax.optimization_barrier((far_texts, outer, ahead, behind))
     near = (ahead, behind, outer, inner)
     far_slopes, far_grad, sums = call(
         far_kernel,

time: 156 us -> 149 us (0.955)
  starting transfers between devices: 80.8 us -> 60.9 us
  waiting for transfers between devices: 14.3 us -> 26.8 us
    ppermute x10, starting transfers between devices: 74.6 us -> 54.4 us  [moved(): return lax.ppermute(value, ('x', 'y', 'half'), pairs)]
    ppermute x10, waiting for transfers between devices: 11.8 us -> 24.3 us  [moved(): return lax.ppermute(value, ('x', 'y', 'half'), pairs)]
  transfers between devices with their start and end apart: 11 -> 11, of which waited for: 2 -> 3; matrix products, arithmetic and copies ran while one was open for 3% -> 3% of each run, Pallas kernels for 7% -> 8%
where the time goes in v5:
time: 149 us; the launch traced here: 148 us
  starting transfers between devices  60.9 us (41%)
  blocking collectives  35 us (23%)
  waiting for transfers between devices  26.8 us (18%)
  Pallas kernels  11.2 us (8%)
  between operations  5.62 us (4%)
  local copies, waits for them, and re-layouts  4.6 us (3%)
  other arithmetic  4.06 us (3%)
    ppermute x10, starting transfers between devices, moved(): return lax.ppermute(value, ('x', 'y', 'half'), pairs)  54.4 us
    all_to_all x1, blocking collectives, local(): column_rows = lax.all_to_all(row_copies, ('half', 'grp'), 0, 0, tiled=True)  35 us
    ppermute x10, waiting for transfers between devices, moved(): return lax.ppermute(value, ('x', 'y', 'half'), pairs)  24.3 us
    pallas_call x4, Pallas kernels, call(): pl.pallas_call(kernel, out_shape=outs, in_specs=[SMEM] * in_smem + [VMEM]...  10.6 us
    all_to_all x1, starting transfers between devices, local(): lax.all_to_all(row_copies, ('x', 'y'), 0, 0, tiled=True)  6.56 us
    unnamed x14, local copies, waits for them, and re-layouts  4.01 us
    convert_element_type x1, other arithmetic, local(): image_grad = (scale * image_sum).astype(BF16)  3 us
  transfers between devices with their start and end apart: 11, of which 3 were waited for; matrix products, arithmetic and copies ran while one was open for 3% of the time, Pallas kernels for 8%

profile of v5, /device:TPU:1, one launch (start us, length us, event | category | flops | bytes accessed | tf_op | source)
XLA Modules:
  0.0 148.1 jit_solution(13178496476228280586)
XLA Ops:
  0.6 16.3 %collective-permute-start = (bf16[256,1152]{1,0:T(8,128)(2,1)}, bf16[256,1152]{1,0:T(8,128)(2,1)S(1)}, u32[]{:S(2)}, u32[]{:S(2)}) collective-permute-start(bf16[256,1152]{1,0:T(8,128)(2,1)} %texts.3), channel_id=1, source_target_pairs={{0,16},{16,0},{32,48},{48,32},{64,80},{80,64},{96,112},{112,96},{1... | collective-permute-start | bytes 1769480 | tf_op jit(solution)/shard_map/ppermute | solution.py:121
  16.9 3.2 %collective-permute-start.3 = (bf16[256,1152]{1,0:T(8,128)(2,1)}, bf16[256,1152]{1,0:T(8,128)(2,1)S(1)}, u32[]{:S(2)}, u32[]{:S(2)}) collective-permute-start(bf16[256,1152]{1,0:T(8,128)(2,1)} %mine.3), channel_id=1, source_target_pairs={{0,32},{16,48},{32,64},{48,80},{64,96},{80,112},{96,128},{112,144}... | collective-permute-start | bytes 1769480 | tf_op jit(solution)/shard_map/ppermute | solution.py:121
  20.1 5.6 %collective-permute-start.2 = (bf16[256,1152]{1,0:T(8,128)(2,1)}, bf16[256,1152]{1,0:T(8,128)(2,1)S(1)}, u32[]{:S(2)}, u32[]{:S(2)}) collective-permute-start(bf16[256,1152]{1,0:T(8,128)(2,1)} %mine.3), channel_id=1, source_target_pairs={{0,480},{16,496},{32,0},{48,16},{64,32},{80,48},{96,64},{112,80},{... | collective-permute-start | bytes 1769480 | tf_op jit(solution)/shard_map/ppermute | solution.py:121
  25.7 3.5 %collective-permute-start.1 = (bf16[256,1152]{1,0:T(8,128)(2,1)}, bf16[256,1152]{1,0:T(8,128)(2,1)S(1)}, u32[]{:S(2)}, u32[]{:S(2)}) collective-permute-start(bf16[256,1152]{1,0:T(8,128)(2,1)} %mine.3), channel_id=1, source_target_pairs={{0,448},{16,80},{32,480},{48,112},{64,0},{80,144},{96,32},{112,176... | collective-permute-start | bytes 1769480 | tf_op jit(solution)/shard_map/ppermute | solution.py:121
  29.2 3.2 %collective-permute-start.4 = (bf16[256,1152]{1,0:T(8,128)(2,1)}, bf16[256,1152]{1,0:T(8,128)(2,1)S(1)}, u32[]{:S(2)}, u32[]{:S(2)}) collective-permute-start(bf16[256,1152]{1,0:T(8,128)(2,1)} %mine.3), channel_id=1, source_target_pairs={{448,0},{80,16},{480,32},{112,48},{0,64},{144,80},{32,96},{176,112... | collective-permute-start | bytes 1769480 | tf_op jit(solution)/shard_map/ppermute | solution.py:121
  33.8 0.1 pad_maximum_fusion.scalars
  33.9 0.0 copy-start.3
  33.9 1.1 copy-done.3
  35.0 0.0 copy-start.5
  35.0 1.1 copy-done.5
  36.0 0.0 copy-start.6
  36.0 1.5 first_pair.1
  37.5 0.0 collective-permute-done.texts.far_texts
  37.5 0.0 copy-start.2
  37.5 0.0 collective-permute-done.3.behind
  37.5 6.5 %collective-permute-done.2.ahead = bf16[256,1152]{1,0:T(8,128)(2,1)S(1)} collective-permute-done((bf16[256,1152]{1,0:T(8,128)(2,1)}, bf16[256,1152]{1,0:T(8,128)(2,1)S(1)}, u32[]{:S(2)}, u32[]{:S(2)}) %collective-permute-start.2) | collective-permute-done | bytes 589856 | tf_op jit(solution)/shard_map/ppermute | solution.py:121
  44.1 17.8 %collective-permute-done.1.outer = bf16[256,1152]{1,0:T(8,128)(2,1)S(1)} collective-permute-done((bf16[256,1152]{1,0:T(8,128)(2,1)}, bf16[256,1152]{1,0:T(8,128)(2,1)S(1)}, u32[]{:S(2)}, u32[]{:S(2)}) %collective-permute-start.1) | collective-permute-done | bytes 589856 | tf_op jit(solution)/shard_map/ppermute | solution.py:121
  61.8 0.0 copy-done.6
  61.9 0.0 copy-start.4
  61.9 2.9 %far_pairs.1 = (bf16[4,256,256]{2,1,0:T(8,128)(2,1)S(1)}, bf16[256,1152]{1,0:T(8,128)(2,1)S(1)}, f32[16,256]{1,0:T(8,128)S(1)}) custom-call(f32[2]{0:T(128)S(1)} %pad_maximum_fusion.scalars, bf16[256,1152]{1,0:T(8,128)(2,1)S(1)} %collective-permute-done.texts.far_texts, bf16[256,1152]{1,0:T(8,128)(2,1)S(1)} %copy-done.6, ...), custom_call_target="tpu_custom_call" | custom-call | bytes 589824 | tf_op jit(solution)/shard_map/far_pairs/pallas_call | solution.py:100
  64.8 0.0 copy-done.2
  64.8 1.9 %collective-permute-start.9 = (bf16[256,1152]{1,0:T(8,128)(2,1)S(1)}, bf16[256,1152]{1,0:T(8,128)(2,1)S(1)}, u32[]{:S(2)}, u32[]{:S(2)}) collective-permute-start(bf16[256,1152]{1,0:T(8,128)(2,1)S(1)} %get-tuple-element.46), channel_id=1, source_target_pairs={{0,16},{16,0},{32,48},{48,32},{64,80},{80,64},{96,112},{112,96},{1... | collective-permute-start | bytes 1769480 | tf_op jit(solution)/shard_map/ppermute | solution.py:121
  66.7 0.0 collective-permute-done.4.inner
  66.7 0.0 copy-start
  66.7 0.8 copy-done
  67.5 0.0 copy-done.4
  67.5 5.3 %image_parts.1 = (bf16[4,256,256]{2,1,0:T(8,128)(2,1)S(1)}, f32[32,128]{1,0:T(8,128)S(1)}, f32[256,1152]{1,0:T(8,128)}, bf16[256,1152]{1,0:T(8,128)(2,1)S(1)}, b...) custom-call(f32[2]{0:T(128)S(1)} %pad_maximum_fusion.scalars, ...), custom_call_target="tpu_custom_call" | custom-call | bytes 589824 | tf_op jit(solution)/shard_map/image_parts/pallas_call | solution.py:100
  72.9 4.2 %collective-permute-start.5 = (bf16[256,1152]{1,0:T(8,128)(2,1)S(1)}, bf16[256,1152]{1,0:T(8,128)(2,1)S(1)}, u32[]{:S(2)}, u32[]{:S(2)}) collective-permute-start(bf16[256,1152]{1,0:T(8,128)(2,1)S(1)} %get-tuple-element.38), channel_id=1, source_target_pairs={{480,0},{496,16},{0,32},{16,48},{32,64},{48,80},{64,96},{80,112},{... | collective-permute-start | bytes 1769480 | tf_op jit(solution)/shard_map/ppermute | solution.py:121
  77.1 7.5 %collective-permute-start.6 = (bf16[256,1152]{1,0:T(8,128)(2,1)}, bf16[256,1152]{1,0:T(8,128)(2,1)}, u32[]{:S(2)}, u32[]{:S(2)}) collective-permute-start(bf16[256,1152]{1,0:T(8,128)(2,1)} %get-tuple-element.39), channel_id=1, source_target_pairs={{32,0},{48,16},{64,32},{80,48},{96,64},{112,80},{128,96},{144,112}... | collective-permute-start | bytes 1769480 | tf_op jit(solution)/shard_map/ppermute | solution.py:121
  84.6 1.9 %collective-permute-start.7 = (bf16[256,1152]{1,0:T(8,128)(2,1)S(1)}, bf16[256,1152]{1,0:T(8,128)(2,1)}, u32[]{:S(2)}, u32[]{:S(2)}) collective-permute-start(bf16[256,1152]{1,0:T(8,128)(2,1)S(1)} %get-tuple-element.40), channel_id=1, source_target_pairs={{448,0},{80,16},{480,32},{112,48},{0,64},{144,80},{32,96},{176,112... | collective-permute-start | bytes 1769480 | tf_op jit(solution)/shard_map/ppermute | solution.py:121
  86.6 7.0 %collective-permute-start.8 = (bf16[256,1152]{1,0:T(8,128)(2,1)S(1)}, bf16[256,1152]{1,0:T(8,128)(2,1)}, u32[]{:S(2)}, u32[]{:S(2)}) collective-permute-start(bf16[256,1152]{1,0:T(8,128)(2,1)S(1)} %get-tuple-element.41), channel_id=1, source_target_pairs={{0,448},{16,80},{32,480},{48,112},{64,0},{80,144},{96,32},{112,176... | collective-permute-start | bytes 1769480 | tf_op jit(solution)/shard_map/ppermute | solution.py:121
  93.5 0.0 copy-start.1
  93.6 1.1 copy-done.1
  94.6 0.8 own_texts.1
  95.5 35.0 %all_to_all.20 = f32[32,1,128]{2,1,0:T(1,128)S(1)} all-to-all(f32[32,1,128]{2,1,0:T(1,128)S(1)} %bitcast.11), channel_id=1, replica_groups=mesh['x'=4,'y'=4,'half'=2,'grp'=16] {'half','grp'}, dimensions={0} | all-to-all | bytes 32768 | tf_op jit(solution)/shard_map/all_to_all | solution.py:169
  130.4 0.0 collective-permute-done.9.refs_0_
  130.4 0.0 collective-permute-done.5.refs_1_
  130.4 0.6 column_sums.1
  131.0 6.6 %all-to-all-start.1 = ((f32[16,1,128]{2,1,0:T(1,128)}), f32[16,1,128]{2,1,0:T(1,128)S(1)}, u32[]{:S(2)}, u32[]{:S(2)}) async-start(f32[16,1,128]{2,1,0:T(1,128)} %bitcast.5), calls=%async_computation.1 | async-start | bytes 16384 | tf_op jit(solution)/shard_map/all_to_all | solution.py:178
  137.6 0.0 collective-permute-done.6
  137.6 0.0 collective-permute-done.7
  137.6 0.0 collective-permute-done.8
  137.6 3.0 %multiply_convert_fusion.1 = bf16[256,1152]{1,0:T(8,128)(2,1)} fusion(bf16[256,1152]{1,0:T(8,128)(2,1)} %collective-permute-done.8, bf16[256,1152]{1,0:T(8,128)(2,1)} %collective-permute-done.7, bf16[256,1152]{1,0:T(8,128)(2,1)} %collective-permute-done.6, f32[256,1152]{1,0:T(8,128)} %get-tuple-element.37, ...), kind=kLoop, calls=%fused_computation.1 | loop fusion | flops 2949120 | bytes 4128772 | tf_op jit(solution)/shard_map/convert_element_type | solution.py:187
  140.6 1.0 multiply_convert_fusion
  141.6 2.4 %all-to-all-done.1 = f32[16,1,128]{2,1,0:T(1,128)S(1)} async-done(((f32[16,1,128]{2,1,0:T(1,128)}), f32[16,1,128]{2,1,0:T(1,128)S(1)}, u32[]{:S(2)}, u32[]{:S(2)}) %all-to-all-start.1) | async-done | bytes 8224 | tf_op jit(solution)/shard_map/all_to_all | solution.py:178
  144.0 0.6 fusion
  (1 shorter events, 0.0 us)
Async XLA Ops:
  0.6 36.9 %collective-permute-start = (bf16[256,1152]{1,0:T(8,128)(2,1)}, bf16[256,1152]{1,0:T(8,128)(2,1)S(1)}, u32[]{:S(2)}, u32[]{:S(2)}) collective-permute-start(bf16[256,1152]{1,0:T(8,128)(2,1)} %texts.3), channel_id=1, source_target_pairs={{0,16},{16,0},{32,48},{48,32},{64,80},{80,64},{96,112},{112,96},{1... | collective-permute-start | bytes 1769480 | tf_op jit(solution)/shard_map/ppermute | solution.py:121
  16.9 20.6 %collective-permute-start.3 = (bf16[256,1152]{1,0:T(8,128)(2,1)}, bf16[256,1152]{1,0:T(8,128)(2,1)S(1)}, u32[]{:S(2)}, u32[]{:S(2)}) collective-permute-start(bf16[256,1152]{1,0:T(8,128)(2,1)} %mine.3), channel_id=1, source_target_pairs={{0,32},{16,48},{32,64},{48,80},{64,96},{80,112},{96,128},{112,144}... | collective-permute-start | bytes 1769480 | tf_op jit(solution)/shard_map/ppermute | solution.py:121
  20.1 23.9 %collective-permute-start.2 = (bf16[256,1152]{1,0:T(8,128)(2,1)}, bf16[256,1152]{1,0:T(8,128)(2,1)S(1)}, u32[]{:S(2)}, u32[]{:S(2)}) collective-permute-start(bf16[256,1152]{1,0:T(8,128)(2,1)} %mine.3), channel_id=1, source_target_pairs={{0,480},{16,496},{32,0},{48,16},{64,32},{80,48},{96,64},{112,80},{... | collective-permute-start | bytes 1769480 | tf_op jit(solution)/shard_map/ppermute | solution.py:121
  25.7 36.2 %collective-permute-start.1 = (bf16[256,1152]{1,0:T(8,128)(2,1)}, bf16[256,1152]{1,0:T(8,128)(2,1)S(1)}, u32[]{:S(2)}, u32[]{:S(2)}) collective-permute-start(bf16[256,1152]{1,0:T(8,128)(2,1)} %mine.3), channel_id=1, source_target_pairs={{0,448},{16,80},{32,480},{48,112},{64,0},{80,144},{96,32},{112,176... | collective-permute-start | bytes 1769480 | tf_op jit(solution)/shard_map/ppermute | solution.py:121
  29.2 37.5 %collective-permute-start.4 = (bf16[256,1152]{1,0:T(8,128)(2,1)}, bf16[256,1152]{1,0:T(8,128)(2,1)S(1)}, u32[]{:S(2)}, u32[]{:S(2)}) collective-permute-start(bf16[256,1152]{1,0:T(8,128)(2,1)} %mine.3), channel_id=1, source_target_pairs={{448,0},{80,16},{480,32},{112,48},{0,64},{144,80},{32,96},{176,112... | collective-permute-start | bytes 1769480 | tf_op jit(solution)/shard_map/ppermute | solution.py:121
  33.9 1.1 copy-start.3
  35.0 1.1 copy-start.5
  36.0 25.8 %copy-start.6 = (bf16[256,1152]{1,0:T(8,128)(2,1)S(1)}, bf16[256,1152]{1,0:T(8,128)(2,1)}, u32[]{:S(2)}) copy-start(bf16[256,1152]{1,0:T(8,128)(2,1)} %mine.3) | copy-start | bytes 1769476
  37.5 27.3 %copy-start.2 = (bf16[256,1152]{1,0:T(8,128)(2,1)}, bf16[256,1152]{1,0:T(8,128)(2,1)S(1)}, u32[]{:S(2)}) copy-start(bf16[256,1152]{1,0:T(8,128)(2,1)S(1)} %collective-permute-done.texts.far_texts) | copy-start | bytes 1769476
  61.9 5.7 %copy-start.4 = (bf16[256,1152]{1,0:T(8,128)(2,1)S(1)}, bf16[256,1152]{1,0:T(8,128)(2,1)}, u32[]{:S(2)}) copy-start(bf16[256,1152]{1,0:T(8,128)(2,1)} %texts.3) | copy-start | bytes 1769476
  64.8 65.6 %collective-permute-start.9 = (bf16[256,1152]{1,0:T(8,128)(2,1)S(1)}, bf16[256,1152]{1,0:T(8,128)(2,1)S(1)}, u32[]{:S(2)}, u32[]{:S(2)}) collective-permute-start(bf16[256,1152]{1,0:T(8,128)(2,1)S(1)} %get-tuple-element.46), channel_id=1, source_target_pairs={{0,16},{16,0},{32,48},{48,32},{64,80},{80,64},{96,112},{112,96},{1... | collective-permute-start | bytes 1769480 | tf_op jit(solution)/shard_map/ppermute | solution.py:121
  66.7 0.8 copy-start
  72.9 57.5 %collective-permute-start.5 = (bf16[256,1152]{1,0:T(8,128)(2,1)S(1)}, bf16[256,1152]{1,0:T(8,128)(2,1)S(1)}, u32[]{:S(2)}, u32[]{:S(2)}) collective-permute-start(bf16[256,1152]{1,0:T(8,128)(2,1)S(1)} %get-tuple-element.38), channel_id=1, source_target_pairs={{480,0},{496,16},{0,32},{16,48},{32,64},{48,80},{64,96},{80,112},{... | collective-permute-start | bytes 1769480 | tf_op jit(solution)/shard_map/ppermute | solution.py:121
  77.1 60.5 %collective-permute-start.6 = (bf16[256,1152]{1,0:T(8,128)(2,1)}, bf16[256,1152]{1,0:T(8,128)(2,1)}, u32[]{:S(2)}, u32[]{:S(2)}) collective-permute-start(bf16[256,1152]{1,0:T(8,128)(2,1)} %get-tuple-element.39), channel_id=1, source_target_pairs={{32,0},{48,16},{64,32},{80,48},{96,64},{112,80},{128,96},{144,112}... | collective-permute-start | bytes 1769480 | tf_op jit(solution)/shard_map/ppermute | solution.py:121
  84.6 53.0 %collective-permute-start.7 = (bf16[256,1152]{1,0:T(8,128)(2,1)S(1)}, bf16[256,1152]{1,0:T(8,128)(2,1)}, u32[]{:S(2)}, u32[]{:S(2)}) collective-permute-start(bf16[256,1152]{1,0:T(8,128)(2,1)S(1)} %get-tuple-element.40), channel_id=1, source_target_pairs={{448,0},{80,16},{480,32},{112,48},{0,64},{144,80},{32,96},{176,112... | collective-permute-start | bytes 1769480 | tf_op jit(solution)/shard_map/ppermute | solution.py:121
  86.6 51.1 %collective-permute-start.8 = (bf16[256,1152]{1,0:T(8,128)(2,1)S(1)}, bf16[256,1152]{1,0:T(8,128)(2,1)}, u32[]{:S(2)}, u32[]{:S(2)}) collective-permute-start(bf16[256,1152]{1,0:T(8,128)(2,1)S(1)} %get-tuple-element.41), channel_id=1, source_target_pairs={{0,448},{16,80},{32,480},{48,112},{64,0},{80,144},{96,32},{112,176... | collective-permute-start | bytes 1769480 | tf_op jit(solution)/shard_map/ppermute | solution.py:121
  93.5 1.1 copy-start.1
  131.0 13.0 %all-to-all-start.1 = ((f32[16,1,128]{2,1,0:T(1,128)}), f32[16,1,128]{2,1,0:T(1,128)S(1)}, u32[]{:S(2)}, u32[]{:S(2)}) async-start(f32[16,1,128]{2,1,0:T(1,128)} %bitcast.5), calls=%async_computation.1 | async-start | bytes 16384 | tf_op jit(solution)/shard_map/all_to_all | solution.py:178

commit v6 on v5

--- a/solution.py
+++ b/solution.py
@@ -174,7 +174,7 @@
         out_specs=VMEM,
         compiler_params=PARAMS,
         name="column_sums",
-    )(column_rows, text_back, image_back[0])
+    )(column_rows, text_back, image_back[1])
     sums_all = jnp.sum(lax.all_to_all(row_copies, ("x", "y"), 0, 0, tiled=True), axis=0)
 
     batch_rows = rows * columns_count * in_column

time: 149 us -> 151 us (1.013)
  the two profiles are of different devices: /device:TPU:1 before, /device:TPU:32 now
where the time goes in v6:
time: 151 us
  starting transfers between devices  69.7 us (46%)
  waiting for transfers between devices  36.4 us (24%)
  blocking collectives  19.2 us (13%)
  Pallas kernels  11.2 us (7%)
  between operations  5.62 us (4%)
  local copies, waits for them, and re-layouts  4.6 us (3%)
  other arithmetic  4.02 us (3%)
    ppermute x10, starting transfers between devices, moved(): return lax.ppermute(value, ('x', 'y', 'half'), pairs)  62.1 us
    ppermute x10, waiting for transfers between devices, moved(): return lax.ppermute(value, ('x', 'y', 'half'), pairs)  36.4 us
    all_to_all x1, blocking collectives, local(): column_rows = lax.all_to_all(row_copies, ('half', 'grp'), 0, 0, tiled=True)  19.2 us
    pallas_call x4, Pallas kernels, call(): pl.pallas_call(kernel, out_shape=outs, in_specs=[SMEM] * in_smem + [VMEM]...  10.6 us
    all_to_all x1, starting transfers between devices, local(): lax.all_to_all(row_copies, ('x', 'y'), 0, 0, tiled=True)  7.64 us
    unnamed x14, local copies, waits for them, and re-layouts  4.01 us
  transfers between devices with their start and end apart: 11, of which 2 were waited for; matrix products, arithmetic and copies ran while one was open for 3% of the time, Pallas kernels for 7%

profile of v6, /device:TPU:32, one launch (start us, length us, event | category | flops | bytes accessed | tf_op | source)
XLA Modules:
  0.0 150.8 jit_solution(12857133745849875517)
XLA Ops:
  0.6 14.8 %collective-permute-start = (bf16[256,1152]{1,0:T(8,128)(2,1)}, bf16[256,1152]{1,0:T(8,128)(2,1)S(1)}, u32[]{:S(2)}, u32[]{:S(2)}) collective-permute-start(bf16[256,1152]{1,0:T(8,128)(2,1)} %texts.3), channel_id=1, source_target_pairs={{0,16},{16,0},{32,48},{48,32},{64,80},{80,64},{96,112},{112,96},{1... | collective-permute-start | bytes 1769480 | tf_op jit(solution)/shard_map/ppermute | solution.py:121
  15.5 3.5 %collective-permute-start.3 = (bf16[256,1152]{1,0:T(8,128)(2,1)}, bf16[256,1152]{1,0:T(8,128)(2,1)S(1)}, u32[]{:S(2)}, u32[]{:S(2)}) collective-permute-start(bf16[256,1152]{1,0:T(8,128)(2,1)} %mine.3), channel_id=1, source_target_pairs={{0,32},{16,48},{32,64},{48,80},{64,96},{80,112},{96,128},{112,144}... | collective-permute-start | bytes 1769480 | tf_op jit(solution)/shard_map/ppermute | solution.py:121
  19.0 5.7 %collective-permute-start.2 = (bf16[256,1152]{1,0:T(8,128)(2,1)}, bf16[256,1152]{1,0:T(8,128)(2,1)S(1)}, u32[]{:S(2)}, u32[]{:S(2)}) collective-permute-start(bf16[256,1152]{1,0:T(8,128)(2,1)} %mine.3), channel_id=1, source_target_pairs={{0,480},{16,496},{32,0},{48,16},{64,32},{80,48},{96,64},{112,80},{... | collective-permute-start | bytes 1769480 | tf_op jit(solution)/shard_map/ppermute | solution.py:121
  24.6 4.0 %collective-permute-start.1 = (bf16[256,1152]{1,0:T(8,128)(2,1)}, bf16[256,1152]{1,0:T(8,128)(2,1)S(1)}, u32[]{:S(2)}, u32[]{:S(2)}) collective-permute-start(bf16[256,1152]{1,0:T(8,128)(2,1)} %mine.3), channel_id=1, source_target_pairs={{0,448},{16,80},{32,480},{48,112},{64,0},{80,144},{96,32},{112,176... | collective-permute-start | bytes 1769480 | tf_op jit(solution)/shard_map/ppermute | solution.py:121
  28.6 3.4 %collective-permute-start.4 = (bf16[256,1152]{1,0:T(8,128)(2,1)}, bf16[256,1152]{1,0:T(8,128)(2,1)S(1)}, u32[]{:S(2)}, u32[]{:S(2)}) collective-permute-start(bf16[256,1152]{1,0:T(8,128)(2,1)} %mine.3), channel_id=1, source_target_pairs={{448,0},{80,16},{480,32},{112,48},{0,64},{144,80},{32,96},{176,112... | collective-permute-start | bytes 1769480 | tf_op jit(solution)/shard_map/ppermute | solution.py:121
  33.3 0.1 pad_maximum_fusion.scalars
  33.4 0.0 copy-start.3
  33.4 1.1 copy-done.3
  34.5 0.0 copy-start.5
  34.5 1.1 copy-done.5
  35.5 0.0 copy-start.6
  35.6 1.5 first_pair.1
  37.0 30.1 %collective-permute-done.texts.far_texts = bf16[256,1152]{1,0:T(8,128)(2,1)S(1)} collective-permute-done((bf16[256,1152]{1,0:T(8,128)(2,1)}, bf16[256,1152]{1,0:T(8,128)(2,1)S(1)}, u32[]{:S(2)}, u32[]{:S(2)}) %collective-permute-start) | collective-permute-done | bytes 589856 | tf_op jit(solution)/shard_map/ppermute | solution.py:121
  67.2 0.0 copy-start.2
  67.2 0.0 collective-permute-done.3.behind
  67.2 0.0 collective-permute-done.2.ahead
  67.2 0.0 collective-permute-done.1.outer
  67.2 0.0 copy-done.6
  67.2 0.0 copy-start.4
  67.2 2.9 %far_pairs.1 = (bf16[4,256,256]{2,1,0:T(8,128)(2,1)S(1)}, bf16[256,1152]{1,0:T(8,128)(2,1)S(1)}, f32[16,256]{1,0:T(8,128)S(1)}) custom-call(f32[2]{0:T(128)S(1)} %pad_maximum_fusion.scalars, bf16[256,1152]{1,0:T(8,128)(2,1)S(1)} %collective-permute-done.texts.far_texts, bf16[256,1152]{1,0:T(8,128)(2,1)S(1)} %copy-done.6, ...), custom_call_target="tpu_custom_call" | custom-call | bytes 589824 | tf_op jit(solution)/shard_map/far_pairs/pallas_call | solution.py:100
  70.1 0.0 copy-done.2
  70.1 12.1 %collective-permute-start.9 = (bf16[256,1152]{1,0:T(8,128)(2,1)S(1)}, bf16[256,1152]{1,0:T(8,128)(2,1)S(1)}, u32[]{:S(2)}, u32[]{:S(2)}) collective-permute-start(bf16[256,1152]{1,0:T(8,128)(2,1)S(1)} %get-tuple-element.46), channel_id=1, source_target_pairs={{0,16},{16,0},{32,48},{48,32},{64,80},{80,64},{96,112},{112,96},{1... | collective-permute-start | bytes 1769480 | tf_op jit(solution)/shard_map/ppermute | solution.py:121
  82.3 0.0 collective-permute-done.4.inner
  82.3 0.0 copy-start
  82.3 0.8 copy-done
  83.1 0.0 copy-done.4
  83.1 5.3 %image_parts.1 = (bf16[4,256,256]{2,1,0:T(8,128)(2,1)S(1)}, f32[32,128]{1,0:T(8,128)S(1)}, f32[256,1152]{1,0:T(8,128)}, bf16[256,1152]{1,0:T(8,128)(2,1)}, bf16[...) custom-call(f32[2]{0:T(128)S(1)} %pad_maximum_fusion.scalars, ...), custom_call_target="tpu_custom_call" | custom-call | bytes 589824 | tf_op jit(solution)/shard_map/image_parts/pallas_call | solution.py:100
  88.4 7.3 %collective-permute-start.6 = (bf16[256,1152]{1,0:T(8,128)(2,1)S(1)}, bf16[256,1152]{1,0:T(8,128)(2,1)S(1)}, u32[]{:S(2)}, u32[]{:S(2)}) collective-permute-start(bf16[256,1152]{1,0:T(8,128)(2,1)S(1)} %get-tuple-element.39), channel_id=1, source_target_pairs={{32,0},{48,16},{64,32},{80,48},{96,64},{112,80},{128,96},{144,112}... | collective-permute-start | bytes 1769480 | tf_op jit(solution)/shard_map/ppermute | solution.py:121
  95.7 1.9 %collective-permute-start.5 = (bf16[256,1152]{1,0:T(8,128)(2,1)}, bf16[256,1152]{1,0:T(8,128)(2,1)}, u32[]{:S(2)}, u32[]{:S(2)}) collective-permute-start(bf16[256,1152]{1,0:T(8,128)(2,1)} %get-tuple-element.38), channel_id=1, source_target_pairs={{480,0},{496,16},{0,32},{16,48},{32,64},{48,80},{64,96},{80,112},{... | collective-permute-start | bytes 1769480 | tf_op jit(solution)/shard_map/ppermute | solution.py:121
  97.6 1.9 %collective-permute-start.7 = (bf16[256,1152]{1,0:T(8,128)(2,1)S(1)}, bf16[256,1152]{1,0:T(8,128)(2,1)}, u32[]{:S(2)}, u32[]{:S(2)}) collective-permute-start(bf16[256,1152]{1,0:T(8,128)(2,1)S(1)} %get-tuple-element.40), channel_id=1, source_target_pairs={{448,0},{80,16},{480,32},{112,48},{0,64},{144,80},{32,96},{176,112... | collective-permute-start | bytes 1769480 | tf_op jit(solution)/shard_map/ppermute | solution.py:121
  99.6 7.5 %collective-permute-start.8 = (bf16[256,1152]{1,0:T(8,128)(2,1)S(1)}, bf16[256,1152]{1,0:T(8,128)(2,1)}, u32[]{:S(2)}, u32[]{:S(2)}) collective-permute-start(bf16[256,1152]{1,0:T(8,128)(2,1)S(1)} %get-tuple-element.41), channel_id=1, source_target_pairs={{0,448},{16,80},{32,480},{48,112},{64,0},{80,144},{96,32},{112,176... | collective-permute-start | bytes 1769480 | tf_op jit(solution)/shard_map/ppermute | solution.py:121
  107.1 0.0 copy-start.1
  107.1 1.1 copy-done.1
  108.2 0.8 own_texts.1
  109.0 19.2 %all_to_all.20 = f32[32,1,128]{2,1,0:T(1,128)S(1)} all-to-all(f32[32,1,128]{2,1,0:T(1,128)S(1)} %bitcast.11), channel_id=1, replica_groups=mesh['x'=4,'y'=4,'half'=2,'grp'=16] {'half','grp'}, dimensions={0} | all-to-all | bytes 32768 | tf_op jit(solution)/shard_map/all_to_all | solution.py:169
  128.3 0.0 collective-permute-done.9.refs_0_
  128.3 0.0 collective-permute-done.6.refs_1_
  128.3 0.6 column_sums.1
  128.9 7.6 %all-to-all-start.1 = ((f32[16,1,128]{2,1,0:T(1,128)}), f32[16,1,128]{2,1,0:T(1,128)S(1)}, u32[]{:S(2)}, u32[]{:S(2)}) async-start(f32[16,1,128]{2,1,0:T(1,128)} %bitcast.5), calls=%async_computation.1 | async-start | bytes 16384 | tf_op jit(solution)/shard_map/all_to_all | solution.py:178
  136.5 0.0 collective-permute-done.5
  136.5 0.0 collective-permute-done.7
  136.5 6.2 %collective-permute-done.8 = bf16[256,1152]{1,0:T(8,128)(2,1)} collective-permute-done((bf16[256,1152]{1,0:T(8,128)(2,1)S(1)}, bf16[256,1152]{1,0:T(8,128)(2,1)}, u32[]{:S(2)}, u32[]{:S(2)}) %collective-permute-start.8) | collective-permute-done | bytes 589856 | tf_op jit(solution)/shard_map/ppermute | solution.py:121
  142.8 3.0 %multiply_convert_fusion.1 = bf16[256,1152]{1,0:T(8,128)(2,1)} fusion(bf16[256,1152]{1,0:T(8,128)(2,1)} %collective-permute-done.8, bf16[256,1152]{1,0:T(8,128)(2,1)} %collective-permute-done.7, bf16[256,1152]{1,0:T(8,128)(2,1)S(1)} %collective-permute-done.6.refs_1_, f32[256,1152]{1,0:T(8,128)} %get-tuple-element.37, ...), kind=kLoop, calls=%fused_computation.1 | loop fusion | flops 2949120 | bytes 4128772 | tf_op jit(solution)/shard_map/convert_element_type | solution.py:187
  145.7 1.0 multiply_convert_fusion
  146.7 0.0 all-to-all-done.1
  146.7 0.6 fusion
  (1 shorter events, 0.0 us)
Async XLA Ops:
  0.6 66.5 %collective-permute-start = (bf16[256,1152]{1,0:T(8,128)(2,1)}, bf16[256,1152]{1,0:T(8,128)(2,1)S(1)}, u32[]{:S(2)}, u32[]{:S(2)}) collective-permute-start(bf16[256,1152]{1,0:T(8,128)(2,1)} %texts.3), channel_id=1, source_target_pairs={{0,16},{16,0},{32,48},{48,32},{64,80},{80,64},{96,112},{112,96},{1... | collective-permute-start | bytes 1769480 | tf_op jit(solution)/shard_map/ppermute | solution.py:121
  15.5 51.7 %collective-permute-start.3 = (bf16[256,1152]{1,0:T(8,128)(2,1)}, bf16[256,1152]{1,0:T(8,128)(2,1)S(1)}, u32[]{:S(2)}, u32[]{:S(2)}) collective-permute-start(bf16[256,1152]{1,0:T(8,128)(2,1)} %mine.3), channel_id=1, source_target_pairs={{0,32},{16,48},{32,64},{48,80},{64,96},{80,112},{96,128},{112,144}... | collective-permute-start | bytes 1769480 | tf_op jit(solution)/shard_map/ppermute | solution.py:121
  19.0 48.2 %collective-permute-start.2 = (bf16[256,1152]{1,0:T(8,128)(2,1)}, bf16[256,1152]{1,0:T(8,128)(2,1)S(1)}, u32[]{:S(2)}, u32[]{:S(2)}) collective-permute-start(bf16[256,1152]{1,0:T(8,128)(2,1)} %mine.3), channel_id=1, source_target_pairs={{0,480},{16,496},{32,0},{48,16},{64,32},{80,48},{96,64},{112,80},{... | collective-permute-start | bytes 1769480 | tf_op jit(solution)/shard_map/ppermute | solution.py:121
  24.6 42.5 %collective-permute-start.1 = (bf16[256,1152]{1,0:T(8,128)(2,1)}, bf16[256,1152]{1,0:T(8,128)(2,1)S(1)}, u32[]{:S(2)}, u32[]{:S(2)}) collective-permute-start(bf16[256,1152]{1,0:T(8,128)(2,1)} %mine.3), channel_id=1, source_target_pairs={{0,448},{16,80},{32,480},{48,112},{64,0},{80,144},{96,32},{112,176... | collective-permute-start | bytes 1769480 | tf_op jit(solution)/shard_map/ppermute | solution.py:121
  28.6 53.6 %collective-permute-start.4 = (bf16[256,1152]{1,0:T(8,128)(2,1)}, bf16[256,1152]{1,0:T(8,128)(2,1)S(1)}, u32[]{:S(2)}, u32[]{:S(2)}) collective-permute-start(bf16[256,1152]{1,0:T(8,128)(2,1)} %mine.3), channel_id=1, source_target_pairs={{448,0},{80,16},{480,32},{112,48},{0,64},{144,80},{32,96},{176,112... | collective-permute-start | bytes 1769480 | tf_op jit(solution)/shard_map/ppermute | solution.py:121
  33.4 1.1 copy-start.3
  34.5 1.1 copy-start.5
  35.5 31.6 %copy-start.6 = (bf16[256,1152]{1,0:T(8,128)(2,1)S(1)}, bf16[256,1152]{1,0:T(8,128)(2,1)}, u32[]{:S(2)}) copy-start(bf16[256,1152]{1,0:T(8,128)(2,1)} %mine.3) | copy-start | bytes 1769476
  67.2 2.9 %copy-start.2 = (bf16[256,1152]{1,0:T(8,128)(2,1)}, bf16[256,1152]{1,0:T(8,128)(2,1)S(1)}, u32[]{:S(2)}) copy-start(bf16[256,1152]{1,0:T(8,128)(2,1)S(1)} %collective-permute-done.texts.far_texts) | copy-start | bytes 1769476
  67.2 15.9 %copy-start.4 = (bf16[256,1152]{1,0:T(8,128)(2,1)S(1)}, bf16[256,1152]{1,0:T(8,128)(2,1)}, u32[]{:S(2)}) copy-start(bf16[256,1152]{1,0:T(8,128)(2,1)} %texts.3) | copy-start | bytes 1769476
  70.1 58.1 %collective-permute-start.9 = (bf16[256,1152]{1,0:T(8,128)(2,1)S(1)}, bf16[256,1152]{1,0:T(8,128)(2,1)S(1)}, u32[]{:S(2)}, u32[]{:S(2)}) collective-permute-start(bf16[256,1152]{1,0:T(8,128)(2,1)S(1)} %get-tuple-element.46), channel_id=1, source_target_pairs={{0,16},{16,0},{32,48},{48,32},{64,80},{80,64},{96,112},{112,96},{1... | collective-permute-start | bytes 1769480 | tf_op jit(solution)/shard_map/ppermute | solution.py:121
  82.3 0.8 copy-start
  88.4 39.8 %collective-permute-start.6 = (bf16[256,1152]{1,0:T(8,128)(2,1)S(1)}, bf16[256,1152]{1,0:T(8,128)(2,1)S(1)}, u32[]{:S(2)}, u32[]{:S(2)}) collective-permute-start(bf16[256,1152]{1,0:T(8,128)(2,1)S(1)} %get-tuple-element.39), channel_id=1, source_target_pairs={{32,0},{48,16},{64,32},{80,48},{96,64},{112,80},{128,96},{144,112}... | collective-permute-start | bytes 1769480 | tf_op jit(solution)/shard_map/ppermute | solution.py:121
  95.7 40.8 %collective-permute-start.5 = (bf16[256,1152]{1,0:T(8,128)(2,1)}, bf16[256,1152]{1,0:T(8,128)(2,1)}, u32[]{:S(2)}, u32[]{:S(2)}) collective-permute-start(bf16[256,1152]{1,0:T(8,128)(2,1)} %get-tuple-element.38), channel_id=1, source_target_pairs={{480,0},{496,16},{0,32},{16,48},{32,64},{48,80},{64,96},{80,112},{... | collective-permute-start | bytes 1769480 | tf_op jit(solution)/shard_map/ppermute | solution.py:121
  97.6 38.9 %collective-permute-start.7 = (bf16[256,1152]{1,0:T(8,128)(2,1)S(1)}, bf16[256,1152]{1,0:T(8,128)(2,1)}, u32[]{:S(2)}, u32[]{:S(2)}) collective-permute-start(bf16[256,1152]{1,0:T(8,128)(2,1)S(1)} %get-tuple-element.40), channel_id=1, source_target_pairs={{448,0},{80,16},{480,32},{112,48},{0,64},{144,80},{32,96},{176,112... | collective-permute-start | bytes 1769480 | tf_op jit(solution)/shard_map/ppermute | solution.py:121
  99.6 43.2 %collective-permute-start.8 = (bf16[256,1152]{1,0:T(8,128)(2,1)S(1)}, bf16[256,1152]{1,0:T(8,128)(2,1)}, u32[]{:S(2)}, u32[]{:S(2)}) collective-permute-start(bf16[256,1152]{1,0:T(8,128)(2,1)S(1)} %get-tuple-element.41), channel_id=1, source_target_pairs={{0,448},{16,80},{32,480},{48,112},{64,0},{80,144},{96,32},{112,176... | collective-permute-start | bytes 1769480 | tf_op jit(solution)/shard_map/ppermute | solution.py:121
  107.1 1.1 copy-start.1
  128.9 17.8 %all-to-all-start.1 = ((f32[16,1,128]{2,1,0:T(1,128)}), f32[16,1,128]{2,1,0:T(1,128)S(1)}, u32[]{:S(2)}, u32[]{:S(2)}) async-start(f32[16,1,128]{2,1,0:T(1,128)} %bitcast.5), calls=%async_computation.1 | async-start | bytes 16384 | tf_op jit(solution)/shard_map/all_to_all | solution.py:178
